TPU v7x, 32 devices: a whole 2x2x4 slice. The times are simulated.
32 devices in a mesh: dp: 8 (over z, y), tensor: 4 (over x, core).
Axes of the slice: x: 2, y: 2, z: 4, core: 2. Of those that a mesh axis runs over, the one named last changes fastest.
Arguments:
- tokens: bfloat16 [4096, 2048], P(('dp', 'tensor')), may hold values from -6 to 6
- segments: int32 [4096], P('dp'), may hold values from 0 to 15, never falling along the last dimension, each value on 1 to 1024 neighbouring positions
- attn_gain: float32 [2, 2048], replicated, may hold values from 0.5 to 1.5
- w_query: bfloat16 [2, 2048, 2048], P(None, 'dp', 'tensor'), may hold values from -0.125 to 0.125
- w_key: bfloat16 [2, 2048, 2048], P(None, 'dp', 'tensor'), may hold values from -0.125 to 0.125
- w_value: bfloat16 [2, 2048, 3456], P(None, 'dp', 'tensor'), may hold values from -0.125 to 0.125
- w_swish: bfloat16 [2, 2048, 3456], P(None, 'dp', 'tensor'), may hold values from -0.125 to 0.125
- w_output: bfloat16 [2, 3456, 2048], P(None, 'tensor', 'dp'), may hold values from -0.109375 to 0.109375
- ffn_gain: float32 [2, 2048], replicated, may hold values from 0.5 to 1.5
- w_gelu: bfloat16 [2, 2048, 3456], P(None, 'dp', 'tensor'), may hold values from -0.125 to 0.125
- w_up: bfloat16 [2, 2048, 3456], P(None, 'dp', 'tensor'), may hold values from -0.125 to 0.125
- w_down: bfloat16 [2, 3456, 2048], P(None, 'tensor', 'dp'), may hold values from -0.109375 to 0.109375
- cotangent: bfloat16 [4096, 2048], P(('dp', 'tensor')), may hold values from -6 to 6
Outputs:
- output: bfloat16 [4096, 2048], P(('dp', 'tensor'))
- input_grad: float32 [4096, 2048], P(('dp', 'tensor'))
- grad_attn_gain: float32 [2, 2048], replicated
- grad_query: float32 [2, 2048, 2048], P(None, 'dp', 'tensor')
- grad_key: float32 [2, 2048, 2048], P(None, 'dp', 'tensor')
- grad_value: float32 [2, 2048, 3456], P(None, 'dp', 'tensor')
- grad_swish: float32 [2, 2048, 3456], P(None, 'dp', 'tensor')
- grad_output: float32 [2, 3456, 2048], P(None, 'tensor', 'dp')
- grad_ffn_gain: float32 [2, 2048], replicated
- grad_gelu: float32 [2, 2048, 3456], P(None, 'dp', 'tensor')
- grad_up: float32 [2, 2048, 3456], P(None, 'dp', 'tensor')
- grad_down: float32 [2, 3456, 2048], P(None, 'tensor', 'dp')
Inputs may be any that keep to these rules, and one draw needn't show every extreme that they name: `segments`: ids never fall along the tokens; each document covers 1 to min(2048, 1024) consecutive tokens, and one covers exactly that many.
All inputs are finite; a program needn't handle non-finite values.
Results may differ from a plain program's by a relative error of at most 0.035.
Values may be sent and summed in bfloat16 or wider, within the bound.
A program may use at most 256 MiB of HBM per device.

v0:
```python
import jax
import jax.numpy as jnp
from jax import lax
from jax.sharding import PartitionSpec as P

HEAD_QK = 256
HEAD_V = 432
LEN = 512


EPS = 1e-06
HEAD_FLOOR = 1.0
CONTRACT_ROWS = (((0,), (0,)), ((), ()))
CONTRACT_COLS = (((1,), (1,)), ((), ()))


def shortened(shard):
    return jax.tree.map(lambda a: a.astype(jnp.bfloat16) if a.dtype == jnp.float32 else a, shard)


def norm_rows(values, gain):
    return values * lax.rsqrt(jnp.mean(values * values, -1, keepdims=True) + EPS) * gain


def norm_heads(values):
    return values * lax.rsqrt(jnp.mean(values * values, -1, keepdims=True) + HEAD_FLOOR)


def gelu_tanh(values):
    return jax.nn.gelu(values, approximate=True)


def rotation(length, width):
    half = width // 2
    place = jnp.arange(length, dtype=jnp.float32)
    freqs = 10000.0 ** (-jnp.arange(half, dtype=jnp.float32) / half)
    angle = place[:, None] * freqs[None, :]
    return (jnp.cos(angle)[:, None, :], jnp.sin(angle)[:, None, :])


def rotate(values, cosine, sine):
    half = values.shape[-1] // 2
    first = values[..., :half]
    second = values[..., half:]
    return jnp.concatenate([first * cosine - second * sine, second * cosine + first * sine], -1)


def rotate_back(grads, cosine, sine):
    half = grads.shape[-1] // 2
    first = grads[..., :half]
    second = grads[..., half:]
    return jnp.concatenate([first * cosine + second * sine, second * cosine - first * sine], -1)


def decay_mask(seg_rows, head_ids, length):
    place = jnp.arange(length, dtype=jnp.int32)
    dist = place[:, None] - place[None, :]
    same = (seg_rows[:, :, None] == seg_rows[:, None, :]) & (dist >= 0)[None]
    rates = jnp.log1p(-(2.0 ** (-5.0 - head_ids)))
    decay = jnp.exp(jnp.maximum(dist, 0).astype(jnp.float32)[None] * rates[:, None, None])
    return jnp.where(same[:, None], decay[None], 0.0)


def weights_of(rotated_query, rotated_key, mask, score_scale):
    unnormalized_scores = (
        jnp.einsum(
            "slhd,smhd->shlm", rotated_query, rotated_key, preferred_element_type=jnp.float32
        )
        * score_scale
    )
    return (unnormalized_scores * mask).astype(jnp.bfloat16)


def gather_rows(rows):
    return lax.all_gather(rows, "tensor", axis=0, tiled=True)


def sum_rows(part):
    return lax.psum_scatter(
        part.astype(jnp.bfloat16), "tensor", scatter_dimension=0, tiled=True
    ).astype(jnp.float32)


def fold_rows(acts, weights):
    pieces = jax.tree.map(lambda a: lax.all_gather(a, "dp", axis=0, tiled=True), shortened(weights))
    return tuple((jnp.dot(acts, p, preferred_element_type=jnp.float32) for p in pieces))


def map_columns(acts, weight):
    return jnp.dot(
        acts, lax.all_gather(weight, "dp", axis=1, tiled=True), preferred_element_type=jnp.float32
    )


def back_rows(grads, weights):
    pieces = lax.all_gather(shortened(weights), "dp", axis=0, tiled=True)
    total = lax.dot_general(grads[0], pieces[0], CONTRACT_COLS, preferred_element_type=jnp.float32)
    for grad, piece in zip(grads[1:], pieces[1:]):
        total = total + lax.dot_general(
            grad, piece, CONTRACT_COLS, preferred_element_type=jnp.float32
        )
    return total


def back_columns(grad, weight):
    return lax.dot_general(
        grad,
        lax.all_gather(weight, "dp", axis=1, tiled=True),
        CONTRACT_COLS,
        preferred_element_type=jnp.float32,
    )


def local(
    tokens,
    segments,
    attn_gain,
    w_query,
    w_key,
    w_value,
    w_swish,
    w_output,
    ffn_gain,
    w_gelu,
    w_up,
    w_down,
    cotangent,
):
    layers = w_query.shape[0]
    heads_dev = w_query.shape[2] // HEAD_QK
    seqs = segments.shape[0] // LEN
    score_scale = HEAD_QK ** (-0.5)
    head_ids = (lax.axis_index("tensor") * heads_dev + jnp.arange(heads_dev)).astype(jnp.float32)
    mask = decay_mask(segments.reshape(seqs, LEN), head_ids, LEN)
    cosine, sine = rotation(LEN, HEAD_QK)
    residual = tokens.astype(jnp.float32)
    saved = []
    for layer in range(layers):
        attn_in = (w_query[layer], w_key[layer], w_value[layer], w_swish[layer])
        ffn_in = (w_gelu[layer], w_up[layer])
        whole_in = attn_in + ffn_in
        whole_out = (w_output[layer], w_down[layer])
        normed = gather_rows(norm_rows(residual, attn_gain[layer]).astype(jnp.bfloat16))
        rows_all = normed.shape[0]
        query, keys, values, swish = fold_rows(normed, attn_in)
        vals = values.astype(jnp.bfloat16).reshape(seqs, LEN, heads_dev, HEAD_V)
        rotated_query = rotate(query.reshape(seqs, LEN, heads_dev, HEAD_QK), cosine, sine).astype(
            jnp.bfloat16
        )
        rotated_key = rotate(keys.reshape(seqs, LEN, heads_dev, HEAD_QK), cosine, sine).astype(
            jnp.bfloat16
        )
        probs = weights_of(rotated_query, rotated_key, mask, score_scale)
        mixed = jnp.einsum("shlm,smhv->slhv", probs, vals, preferred_element_type=jnp.float32)
        zed = norm_heads(mixed).reshape(rows_all, -1)
        gated = (jax.nn.silu(swish) * zed).astype(jnp.bfloat16)
        branch = map_columns(gated, w_output[layer])
        mid = residual + sum_rows(branch)
        normed_ffn = gather_rows(norm_rows(mid, ffn_gain[layer]).astype(jnp.bfloat16))
        gate_pre, up_pre = fold_rows(normed_ffn, ffn_in)
        hidden = (gelu_tanh(gate_pre) * up_pre).astype(jnp.bfloat16)
        branch_ffn = map_columns(hidden, w_down[layer])
        saved.append(
            (
                residual,
                normed,
                rotated_query,
                rotated_key,
                vals,
                swish,
                mixed,
                zed,
                gated,
                mid,
                normed_ffn,
                gate_pre,
                up_pre,
                hidden,
                whole_in,
                whole_out,
            )
        )
        residual = mid + sum_rows(branch_ffn)
    output = residual.astype(jnp.bfloat16)
    grad_res = cotangent.astype(jnp.float32)
    weight_parts = [None] * layers
    attn_gain_parts = [None] * layers
    ffn_gain_parts = [None] * layers
    for layer in reversed(range(layers)):
        (
            x_in,
            normed,
            rotated_query,
            rotated_key,
            vals,
            swish,
            mixed,
            zed,
            gated,
            mid,
            normed_ffn,
            gate_pre,
            up_pre,
            hidden,
            whole_in,
            whole_out,
        ) = saved[layer]
        attn_in = (w_query[layer], w_key[layer], w_value[layer], w_swish[layer])
        ffn_in = (w_gelu[layer], w_up[layer])
        rows_all = normed.shape[0]
        grad_c = gather_rows(grad_res.astype(jnp.bfloat16))
        down_grad = lax.dot_general(
            grad_c, hidden, CONTRACT_ROWS, preferred_element_type=jnp.float32
        )
        grad_hidden = back_columns(grad_c, w_down[layer])
        gelu_val, gelu_activation = jax.vjp(gelu_tanh, gate_pre)
        grad_gate = gelu_activation(grad_hidden * up_pre)[0].astype(jnp.bfloat16)
        grad_upv = (grad_hidden * gelu_val).astype(jnp.bfloat16)
        gelu_grad = lax.dot_general(
            normed_ffn, grad_gate, CONTRACT_ROWS, preferred_element_type=jnp.float32
        )
        up_grad = lax.dot_general(
            normed_ffn, grad_upv, CONTRACT_ROWS, preferred_element_type=jnp.float32
        )
        grad_nf = back_rows((grad_gate, grad_upv), ffn_in)
        _, ffn_norm_fn = jax.vjp(norm_rows, mid, ffn_gain[layer])
        grad_mid_norm, ffn_gain_parts[layer] = ffn_norm_fn(sum_rows(grad_nf))
        grad_mid = grad_res + grad_mid_norm
        grad_b = gather_rows(grad_mid.astype(jnp.bfloat16))
        output_grad_t = lax.dot_general(
            grad_b, gated, CONTRACT_ROWS, preferred_element_type=jnp.float32
        )
        grad_gated = back_columns(grad_b, w_output[layer])
        swish_output, swish_fn = jax.vjp(jax.nn.silu, swish)
        grad_sw = swish_fn(grad_gated * zed)[0].astype(jnp.bfloat16)
        grad_zed = grad_gated * swish_output
        _, head_fn = jax.vjp(norm_heads, mixed)
        grad_mixed = head_fn(grad_zed.reshape(mixed.shape))[0].astype(jnp.bfloat16)
        probs = weights_of(rotated_query, rotated_key, mask, score_scale)
        grad_probs = jnp.einsum(
            "slhv,smhv->shlm", grad_mixed, vals, preferred_element_type=jnp.float32
        )
        grad_raw = (grad_probs * mask).astype(jnp.bfloat16)
        grad_vals = jnp.einsum(
            "shlm,slhv->smhv", probs, grad_mixed, preferred_element_type=jnp.float32
        )
        grad_vals = grad_vals.astype(jnp.bfloat16).reshape(rows_all, -1)
        grad_qrot = (
            jnp.einsum("shlm,smhd->slhd", grad_raw, rotated_key, preferred_element_type=jnp.float32)
            * score_scale
        )
        grad_krot = (
            jnp.einsum(
                "shlm,slhd->smhd", grad_raw, rotated_query, preferred_element_type=jnp.float32
            )
            * score_scale
        )
        grad_q = rotate_back(grad_qrot, cosine, sine).astype(jnp.bfloat16).reshape(rows_all, -1)
        grad_k = rotate_back(grad_krot, cosine, sine).astype(jnp.bfloat16).reshape(rows_all, -1)
        attn_grads = tuple(
            (
                lax.dot_general(normed, g, CONTRACT_ROWS, preferred_element_type=jnp.float32)
                for g in (grad_q, grad_k, grad_vals, grad_sw)
            )
        )
        grad_n = back_rows((grad_q, grad_k, grad_vals, grad_sw), attn_in)
        _, attn_norm_fn = jax.vjp(norm_rows, x_in, attn_gain[layer])
        grad_x_norm, attn_gain_parts[layer] = attn_norm_fn(sum_rows(grad_n))
        grad_res = grad_mid + grad_x_norm
        weight_parts[layer] = jax.tree.map(
            lambda part: part.astype(jnp.float32),
            lax.psum_scatter(
                shortened(attn_grads + (output_grad_t, gelu_grad, up_grad, down_grad)),
                "dp",
                scatter_dimension=0,
                tiled=True,
            ),
        )
    attn_gain_grad, ffn_gain_grad = lax.psum(
        (jnp.stack(attn_gain_parts), jnp.stack(ffn_gain_parts)), ("dp", "tensor")
    )
    grad_query = jnp.stack([p[0] for p in weight_parts])
    grad_key = jnp.stack([p[1] for p in weight_parts])
    grad_value = jnp.stack([p[2] for p in weight_parts])
    grad_swish = jnp.stack([p[3] for p in weight_parts])
    grad_output = jnp.stack([p[4].T for p in weight_parts])
    grad_gelu = jnp.stack([p[5] for p in weight_parts])
    grad_up = jnp.stack([p[6] for p in weight_parts])
    grad_down = jnp.stack([p[7].T for p in weight_parts])
    return (
        output,
        grad_res,
        attn_gain_grad,
        grad_query,
        grad_key,
        grad_value,
        grad_swish,
        grad_output,
        ffn_gain_grad,
        grad_gelu,
        grad_up,
        grad_down,
    )


def solution(mesh):
    in_specs = (
        P(("dp", "tensor"), None),
        P("dp"),
        P(),
        P(None, "dp", "tensor"),
        P(None, "dp", "tensor"),
        P(None, "dp", "tensor"),
        P(None, "dp", "tensor"),
        P(None, "tensor", "dp"),
        P(),
        P(None, "dp", "tensor"),
        P(None, "dp", "tensor"),
        P(None, "tensor", "dp"),
        P(("dp", "tensor"), None),
    )
    out_specs = (
        P(("dp", "tensor"), None),
        P(("dp", "tensor"), None),
        P(),
        P(None, "dp", "tensor"),
        P(None, "dp", "tensor"),
        P(None, "dp", "tensor"),
        P(None, "dp", "tensor"),
        P(None, "tensor", "dp"),
        P(),
        P(None, "dp", "tensor"),
        P(None, "dp", "tensor"),
        P(None, "tensor", "dp"),
    )
    return jax.shard_map(local, mesh=mesh, in_specs=in_specs, out_specs=out_specs, check_vma=False)
```

profile of v0, /device:TPU:0, one launch (start us, length us, event | category | flops | bytes accessed | tf_op | source)
XLA Modules:
  0.0 2852.2 jit_solution(5188499778253758723)
XLA Ops:
  37.0 52.0 %all-gather.63.cloned.1.call-done = bf16[1,2048,512]{2,1,0:T(8,128)(2,1)} async-done(((bf16[1,256,512]{2,1,0:T(8,128)(2,1)}), bf16[1,2048,512]{2,1,0:T(8,128)(2,1)}) %all-gather.63.cloned.1.call-update) | async-done | bytes 2097168 | tf_op jit(solution)/shard_map/all_gather | solution.py:85
  93.0 46.5 %all-gather.61.cloned.1.call-done = bf16[1,2048,512]{2,1,0:T(8,128)(2,1)} async-done(((bf16[1,256,512]{2,1,0:T(8,128)(2,1)}), bf16[1,2048,512]{2,1,0:T(8,128)(2,1)}) %all-gather.61.cloned.1.call-update) | async-done | bytes 2097168 | tf_op jit(solution)/shard_map/all_gather | solution.py:85
  145.6 62.5 %all-gather.59.cloned.1.call-done = bf16[1,2048,864]{1,2,0:T(8,128)(2,1)} async-done(((bf16[1,256,864]{1,2,0:T(8,128)(2,1)}), bf16[1,2048,864]{1,2,0:T(8,128)(2,1)}) %all-gather.59.cloned.1.call-update) | async-done | bytes 3538960 | tf_op jit(solution)/shard_map/all_gather | solution.py:85
  216.3 60.0 %all-gather.57.cloned.1.call-done = bf16[1,2048,864]{1,2,0:T(8,128)(2,1)} async-done(((bf16[1,256,864]{1,2,0:T(8,128)(2,1)}), bf16[1,2048,864]{1,2,0:T(8,128)(2,1)}) %all-gather.57.cloned.1.call-update) | async-done | bytes 3538960 | tf_op jit(solution)/shard_map/all_gather | solution.py:85
  282.9 61.7 %all-gather.65.cloned.1.call-done = bf16[1,864,2048]{2,1,0:T(8,128)(2,1)} async-done(((bf16[1,864,256]{2,1,0:T(8,128)(2,1)}), bf16[1,864,2048]{2,1,0:T(8,128)(2,1)}) %all-gather.65.cloned.1.call-update) | async-done | bytes 3538960 | tf_op jit(solution)/shard_map/all_gather | solution.py:91
  385.9 64.8 %all-gather.67.cloned.1.call-done = bf16[1,2048,864]{1,2,0:T(8,128)(2,1)} async-done(((bf16[1,256,864]{1,2,0:T(8,128)(2,1)}), bf16[1,2048,864]{1,2,0:T(8,128)(2,1)}) %all-gather.67.cloned.1.call-update) | async-done | bytes 3538960 | tf_op jit(solution)/shard_map/all_gather | solution.py:85
  479.6 64.4 %all-gather.69.cloned.1.call-done = bf16[1,2048,864]{1,2,0:T(8,128)(2,1)} async-done(((bf16[1,256,864]{1,2,0:T(8,128)(2,1)}), bf16[1,2048,864]{1,2,0:T(8,128)(2,1)}) %all-gather.69.cloned.1.call-update) | async-done | bytes 3538960 | tf_op jit(solution)/shard_map/all_gather | solution.py:85
  550.6 62.0 %all-gather.71.cloned.1.call-done = bf16[1,864,2048]{2,1,0:T(8,128)(2,1)} async-done(((bf16[1,864,256]{2,1,0:T(8,128)(2,1)}), bf16[1,864,2048]{2,1,0:T(8,128)(2,1)}) %all-gather.71.cloned.1.call-update) | async-done | bytes 3538960 | tf_op jit(solution)/shard_map/all_gather | solution.py:91
  653.0 46.5 %all-gather.79.cloned.1.call-done = bf16[1,2048,512]{2,1,0:T(8,128)(2,1)} async-done(((bf16[1,256,512]{2,1,0:T(8,128)(2,1)}), bf16[1,2048,512]{2,1,0:T(8,128)(2,1)}) %all-gather.79.cloned.1.call-update) | async-done | bytes 2097168 | tf_op jit(solution)/shard_map/all_gather | solution.py:85
  728.5 45.5 %all-gather.77.cloned.1.call-done = bf16[1,2048,512]{2,1,0:T(8,128)(2,1)} async-done(((bf16[1,256,512]{2,1,0:T(8,128)(2,1)}), bf16[1,2048,512]{2,1,0:T(8,128)(2,1)}) %all-gather.77.cloned.1.call-update) | async-done | bytes 2097168 | tf_op jit(solution)/shard_map/all_gather | solution.py:85
  787.0 55.5 %all-gather.75.cloned.1.call-done = bf16[1,2048,864]{1,2,0:T(8,128)(2,1)} async-done(((bf16[1,256,864]{1,2,0:T(8,128)(2,1)}), bf16[1,2048,864]{1,2,0:T(8,128)(2,1)}) %all-gather.75.cloned.1.call-update) | async-done | bytes 3538960 | tf_op jit(solution)/shard_map/all_gather | solution.py:85
  849.6 60.6 %all-gather.73.cloned.1.call-done = bf16[1,2048,864]{1,2,0:T(8,128)(2,1)} async-done(((bf16[1,256,864]{1,2,0:T(8,128)(2,1)}), bf16[1,2048,864]{1,2,0:T(8,128)(2,1)}) %all-gather.73.cloned.1.call-update) | async-done | bytes 3538960 | tf_op jit(solution)/shard_map/all_gather | solution.py:85
  917.0 60.8 %all-gather.81.cloned.1.call-done = bf16[1,864,2048]{2,1,0:T(8,128)(2,1)} async-done(((bf16[1,864,256]{2,1,0:T(8,128)(2,1)}), bf16[1,864,2048]{2,1,0:T(8,128)(2,1)}) %all-gather.81.cloned.1.call-update) | async-done | bytes 3538960 | tf_op jit(solution)/shard_map/all_gather | solution.py:91
  1037.7 69.8 %all-gather.87.cloned.1.call-done = bf16[1,864,2048]{2,1,0:T(8,128)(2,1)} async-done(((bf16[1,864,256]{2,1,0:T(8,128)(2,1)}), bf16[1,864,2048]{2,1,0:T(8,128)(2,1)}) %all-gather.87.cloned.1.call-update) | async-done | bytes 3538960 | tf_op jit(solution)/shard_map/all_gather | solution.py:91
  1113.4 62.2 %all-gather.85.cloned.1.call-done = bf16[1,2048,864]{1,2,0:T(8,128)(2,1)} async-done(((bf16[1,256,864]{1,2,0:T(8,128)(2,1)}), bf16[1,2048,864]{1,2,0:T(8,128)(2,1)}) %all-gather.85.cloned.1.call-update) | async-done | bytes 3538960 | tf_op jit(solution)/shard_map/all_gather | solution.py:85
  1204.4 63.8 %all-gather.83.cloned.1.call-done = bf16[1,2048,864]{1,2,0:T(8,128)(2,1)} async-done(((bf16[1,256,864]{1,2,0:T(8,128)(2,1)}), bf16[1,2048,864]{1,2,0:T(8,128)(2,1)}) %all-gather.83.cloned.1.call-update) | async-done | bytes 3538960 | tf_op jit(solution)/shard_map/all_gather | solution.py:85
  1401.1 32.8 %reduce-scatter.31.cloned.1.call-done = bf16[128,2048]{1,0:T(8,128)(2,1)} async-done(((bf16[512,2048]{1,0:T(8,128)(2,1)}), bf16[128,2048]{1,0:T(8,128)(2,1)}) %reduce-scatter.31.cloned.1.call-update) | async-done | bytes 524304 | tf_op jit(solution)/shard_map/reduce_scatter | solution.py:79
  1635.2 63.1 %reduce-scatter.69.cloned.1.call-done = bf16[256,864]{0,1:T(8,128)(2,1)} async-done(((bf16[2048,864]{0,1:T(8,128)(2,1)}), bf16[256,864]{0,1:T(8,128)(2,1)}) %reduce-scatter.69.cloned.1.call-update) | async-done | bytes 442384 | tf_op jit(solution)/shard_map/reduce_scatter | solution.py:272
  1700.8 80.8 %reduce-scatter.67.cloned.1.call-done = bf16[256,864]{0,1:T(8,128)(2,1)} async-done(((bf16[2048,864]{0,1:T(8,128)(2,1)}), bf16[256,864]{0,1:T(8,128)(2,1)}) %reduce-scatter.67.cloned.1.call-update) | async-done | bytes 442384 | tf_op jit(solution)/shard_map/reduce_scatter | solution.py:272
  1781.6 83.3 %reduce-scatter.65.cloned.1.call-done = bf16[256,864]{0,1:T(8,128)(2,1)} async-done(((bf16[2048,864]{0,1:T(8,128)(2,1)}), bf16[256,864]{0,1:T(8,128)(2,1)}) %reduce-scatter.65.cloned.1.call-update) | async-done | bytes 442384 | tf_op jit(solution)/shard_map/reduce_scatter | solution.py:272
  1867.4 80.6 %reduce-scatter.63.cloned.1.call-done = bf16[256,864]{0,1:T(8,128)(2,1)} async-done(((bf16[2048,864]{0,1:T(8,128)(2,1)}), bf16[256,864]{0,1:T(8,128)(2,1)}) %reduce-scatter.63.cloned.1.call-update) | async-done | bytes 442384 | tf_op jit(solution)/shard_map/reduce_scatter | solution.py:272
  1948.0 83.2 %reduce-scatter.61.cloned.1.call-done = bf16[256,864]{0,1:T(8,128)(2,1)} async-done(((bf16[2048,864]{0,1:T(8,128)(2,1)}), bf16[256,864]{0,1:T(8,128)(2,1)}) %reduce-scatter.61.cloned.1.call-update) | async-done | bytes 442384 | tf_op jit(solution)/shard_map/reduce_scatter | solution.py:272
  2066.6 41.0 %all-reduce = (f32[2,2048]{1,0:T(2,128)}, f32[2,2048]{1,0:T(2,128)}) all-reduce(f32[2,2048]{1,0:T(2,128)S(1)} %pad_maximum_fusion.16, f32[2,2048]{1,0:T(2,128)S(1)} %pad_maximum_fusion.17), channel_id=1, replica_groups=mesh['dp'=8,'tensor'=4] {'dp','tensor'}, use_global_device_ids=true, to_apply=%region_22.23 | all-reduce | flops 8192 | bytes 65536 | tf_op jit(solution)/shard_map/psum | solution.py:279
  2136.5 70.1 %reduce-scatter.41.cloned.1.call-done = bf16[256,512]{1,0:T(8,128)(2,1)} async-done(((bf16[2048,512]{1,0:T(8,128)(2,1)}), bf16[256,512]{1,0:T(8,128)(2,1)}) %reduce-scatter.41.cloned.1.call-update) | async-done | bytes 262160 | tf_op jit(solution)/shard_map/reduce_scatter | solution.py:272
  2208.7 68.2 %reduce-scatter.47.cloned.1.call-done = bf16[256,512]{1,0:T(8,128)(2,1)} async-done(((bf16[2048,512]{1,0:T(8,128)(2,1)}), bf16[256,512]{1,0:T(8,128)(2,1)}) %reduce-scatter.47.cloned.1.call-update) | async-done | bytes 262160 | tf_op jit(solution)/shard_map/reduce_scatter | solution.py:272
  2276.9 70.3 %reduce-scatter.45.cloned.1.call-done = bf16[256,512]{1,0:T(8,128)(2,1)} async-done(((bf16[2048,512]{1,0:T(8,128)(2,1)}), bf16[256,512]{1,0:T(8,128)(2,1)}) %reduce-scatter.45.cloned.1.call-update) | async-done | bytes 262160 | tf_op jit(solution)/shard_map/reduce_scatter | solution.py:272
  2351.0 78.4 %reduce-scatter.59.cloned.1.call-done = bf16[256,864]{0,1:T(8,128)(2,1)} async-done(((bf16[2048,864]{0,1:T(8,128)(2,1)}), bf16[256,864]{0,1:T(8,128)(2,1)}) %reduce-scatter.59.cloned.1.call-update) | async-done | bytes 442384 | tf_op jit(solution)/shard_map/reduce_scatter | solution.py:272
  2429.4 82.6 %reduce-scatter.57.cloned.1.call-done = bf16[256,864]{0,1:T(8,128)(2,1)} async-done(((bf16[2048,864]{0,1:T(8,128)(2,1)}), bf16[256,864]{0,1:T(8,128)(2,1)}) %reduce-scatter.57.cloned.1.call-update) | async-done | bytes 442384 | tf_op jit(solution)/shard_map/reduce_scatter | solution.py:272
  2514.5 80.2 %reduce-scatter.51.cloned.1.call-done = bf16[256,864]{0,1:T(8,128)(2,1)} async-done(((bf16[2048,864]{0,1:T(8,128)(2,1)}), bf16[256,864]{0,1:T(8,128)(2,1)}) %reduce-scatter.51.cloned.1.call-update) | async-done | bytes 442384 | tf_op jit(solution)/shard_map/reduce_scatter | solution.py:272
  2594.7 82.7 %reduce-scatter.49.cloned.1.call-done = bf16[256,864]{0,1:T(8,128)(2,1)} async-done(((bf16[2048,864]{0,1:T(8,128)(2,1)}), bf16[256,864]{0,1:T(8,128)(2,1)}) %reduce-scatter.49.cloned.1.call-update) | async-done | bytes 442384 | tf_op jit(solution)/shard_map/reduce_scatter | solution.py:272
  2679.9 80.3 %reduce-scatter.55.cloned.1.call-done = bf16[256,864]{0,1:T(8,128)(2,1)} async-done(((bf16[2048,864]{0,1:T(8,128)(2,1)}), bf16[256,864]{0,1:T(8,128)(2,1)}) %reduce-scatter.55.cloned.1.call-update) | async-done | bytes 442384 | tf_op jit(solution)/shard_map/reduce_scatter | solution.py:272
  2760.1 82.6 %reduce-scatter.53.cloned.1.call-done = bf16[256,864]{0,1:T(8,128)(2,1)} async-done(((bf16[2048,864]{0,1:T(8,128)(2,1)}), bf16[256,864]{0,1:T(8,128)(2,1)}) %reduce-scatter.53.cloned.1.call-update) | async-done | bytes 442384 | tf_op jit(solution)/shard_map/reduce_scatter | solution.py:272
  (473 shorter events, 737.3 us)
Async XLA Ops:
  12.5 127.1 %all-gather.61.cloned.1.call-start = ((), (), s32[]{:S(2)}) async-start(), calls=%async_computation.58 | async-start | bytes 2359296 | tf_op jit(solution)/shard_map/all_gather | solution.py:85
  13.4 194.7 %all-gather.59.cloned.1.call-start = ((), (), s32[]{:S(2)}) async-start(), calls=%async_computation.57 | async-start | bytes 3981312 | tf_op jit(solution)/shard_map/all_gather | solution.py:85
  14.4 261.9 %all-gather.57.cloned.1.call-start = ((), (), s32[]{:S(2)}) async-start(), calls=%async_computation.56 | async-start | bytes 3981312 | tf_op jit(solution)/shard_map/all_gather | solution.py:85
  15.5 329.1 %all-gather.65.cloned.1.call-start = ((), (), s32[]{:S(2)}) async-start(), calls=%async_computation.60 | async-start | bytes 3981312 | tf_op jit(solution)/shard_map/all_gather | solution.py:91
  16.5 363.7 %reduce-scatter.25.cloned.1.call-start = ((), (), s32[]{:S(2)}) async-start(), calls=%async_computation.25 | async-start | bytes 2621440 | tf_op jit(solution)/shard_map/reduce_scatter | solution.py:79
  383.8 160.2 %all-gather.69.cloned.1.call-start = ((), (), s32[]{:S(2)}) async-start(), calls=%async_computation.62 | async-start | bytes 3981312 | tf_op jit(solution)/shard_map/all_gather | solution.py:85
  384.8 227.8 %all-gather.71.cloned.1.call-start = ((), (), s32[]{:S(2)}) async-start(), calls=%async_computation.63 | async-start | bytes 3981312 | tf_op jit(solution)/shard_map/all_gather | solution.py:91
  385.9 262.2 %reduce-scatter.27.cloned.1.call-start = ((), (), s32[]{:S(2)}) async-start(), calls=%async_computation.27 | async-start | bytes 2621440 | tf_op jit(solution)/shard_map/reduce_scatter | solution.py:79
  651.0 191.4 %all-gather.75.cloned.1.call-start = ((), (), s32[]{:S(2)}) async-start(), calls=%async_computation.65 | async-start | bytes 3981312 | tf_op jit(solution)/shard_map/all_gather | solution.py:85
  651.6 258.5 %all-gather.73.cloned.1.call-start = ((), (), s32[]{:S(2)}) async-start(), calls=%async_computation.64 | async-start | bytes 3981312 | tf_op jit(solution)/shard_map/all_gather | solution.py:85
  652.2 325.6 %all-gather.81.cloned.1.call-start = ((), (), s32[]{:S(2)}) async-start(), calls=%async_computation.68 | async-start | bytes 3981312 | tf_op jit(solution)/shard_map/all_gather | solution.py:91
  652.8 360.8 %reduce-scatter.29.cloned.1.call-start = ((), (), s32[]{:S(2)}) async-start(), calls=%async_computation.29 | async-start | bytes 2621440 | tf_op jit(solution)/shard_map/reduce_scatter | solution.py:79
  985.1 190.4 %all-gather.85.cloned.1.call-start = ((), (), s32[]{:S(2)}) async-start(), calls=%async_computation.70 | async-start | bytes 3981312 | tf_op jit(solution)/shard_map/all_gather | solution.py:85
  985.9 212.7 %all-gather.47.cloned.1.call-start = ((), (), s32[]{:S(2)}) async-start(), calls=%async_computation.30 | async-start | bytes 2621440 | tf_op jit(solution)/shard_map/all_gather | solution.py:75
  1016.9 251.4 %all-gather.83.cloned.1.call-start = ((), (), s32[]{:S(2)}) async-start(), calls=%async_computation.69 | async-start | bytes 3981312 | tf_op jit(solution)/shard_map/all_gather | solution.py:85
  1017.4 295.0 %reduce-scatter.33.cloned.1.call-start = ((), (), s32[]{:S(2)}) async-start(), calls=%async_computation.33 | async-start | bytes 2621440 | tf_op jit(solution)/shard_map/reduce_scatter | solution.py:79
  1514.2 184.2 %reduce-scatter.69.cloned.1.call-start = ((), (), s32[]{:S(2)}) async-start(), calls=%async_computation.54 | async-start | bytes 3981312 | tf_op jit(solution)/shard_map/reduce_scatter | solution.py:272
  1520.8 260.8 %reduce-scatter.67.cloned.1.call-start = ((), (), s32[]{:S(2)}) async-start(), calls=%async_computation.53 | async-start | bytes 3981312 | tf_op jit(solution)/shard_map/reduce_scatter | solution.py:272
  1527.4 337.5 %reduce-scatter.65.cloned.1.call-start = ((), (), s32[]{:S(2)}) async-start(), calls=%async_computation.52 | async-start | bytes 3981312 | tf_op jit(solution)/shard_map/reduce_scatter | solution.py:272
  1534.0 414.0 %reduce-scatter.63.cloned.1.call-start = ((), (), s32[]{:S(2)}) async-start(), calls=%async_computation.51 | async-start | bytes 3981312 | tf_op jit(solution)/shard_map/reduce_scatter | solution.py:272
  1540.6 490.5 %reduce-scatter.61.cloned.1.call-start = ((), (), s32[]{:S(2)}) async-start(), calls=%async_computation.50 | async-start | bytes 3981312 | tf_op jit(solution)/shard_map/reduce_scatter | solution.py:272
  1547.4 517.4 %reduce-scatter.39.cloned.1.call-start = ((), (), s32[]{:S(2)}) async-start(), calls=%async_computation.39 | async-start | bytes 2621440 | tf_op jit(solution)/shard_map/reduce_scatter | solution.py:79
  1575.3 561.3 %reduce-scatter.43.cloned.1.call-start = ((), (), s32[]{:S(2)}) async-start(), calls=%async_computation.41 | async-start | bytes 2359296 | tf_op jit(solution)/shard_map/reduce_scatter | solution.py:272
  1580.5 626.1 %reduce-scatter.41.cloned.1.call-start = ((), (), s32[]{:S(2)}) async-start(), calls=%async_computation.40 | async-start | bytes 2359296 | tf_op jit(solution)/shard_map/reduce_scatter | solution.py:272
  1585.8 691.1 %reduce-scatter.47.cloned.1.call-start = ((), (), s32[]{:S(2)}) async-start(), calls=%async_computation.43 | async-start | bytes 2359296 | tf_op jit(solution)/shard_map/reduce_scatter | solution.py:272
  1591.1 756.1 %reduce-scatter.45.cloned.1.call-start = ((), (), s32[]{:S(2)}) async-start(), calls=%async_computation.42 | async-start | bytes 2359296 | tf_op jit(solution)/shard_map/reduce_scatter | solution.py:272
  1595.4 834.0 %reduce-scatter.59.cloned.1.call-start = ((), (), s32[]{:S(2)}) async-start(), calls=%async_computation.49 | async-start | bytes 3981312 | tf_op jit(solution)/shard_map/reduce_scatter | solution.py:272
  1602.3 909.7 %reduce-scatter.57.cloned.1.call-start = ((), (), s32[]{:S(2)}) async-start(), calls=%async_computation.48 | async-start | bytes 3981312 | tf_op jit(solution)/shard_map/reduce_scatter | solution.py:272
  1608.9 985.8 %reduce-scatter.51.cloned.1.call-start = ((), (), s32[]{:S(2)}) async-start(), calls=%async_computation.45 | async-start | bytes 3981312 | tf_op jit(solution)/shard_map/reduce_scatter | solution.py:272
  1615.5 1061.9 %reduce-scatter.49.cloned.1.call-start = ((), (), s32[]{:S(2)}) async-start(), calls=%async_computation.44 | async-start | bytes 3981312 | tf_op jit(solution)/shard_map/reduce_scatter | solution.py:272
  1622.2 1138.0 %reduce-scatter.55.cloned.1.call-start = ((), (), s32[]{:S(2)}) async-start(), calls=%async_computation.47 | async-start | bytes 3981312 | tf_op jit(solution)/shard_map/reduce_scatter | solution.py:272
  1628.6 1214.1 %reduce-scatter.53.cloned.1.call-start = ((), (), s32[]{:S(2)}) async-start(), calls=%async_computation.46 | async-start | bytes 3981312 | tf_op jit(solution)/shard_map/reduce_scatter | solution.py:272
  (125 other events, 5057.6 us)
Sparse Core Ops, SparseCore 0:
  39.7 49.2 all-gather.62
  91.7 47.7 all-gather.60
  142.0 66.0 all-gather.58
  210.6 65.7 all-gather.56
  278.8 65.7 all-gather.64
  383.1 67.5 all-gather.66
  476.4 67.5 all-gather.68
  546.8 65.7 all-gather.70
  650.2 49.2 all-gather.78
  724.6 49.2 all-gather.76
  776.4 66.0 all-gather.74
  844.4 65.7 all-gather.72
  912.0 65.7 all-gather.80
  1039.9 67.5 all-gather.86
  1109.8 65.7 all-gather.84
  1200.6 67.5 all-gather.82
  1535.6 79.5 reduce-scatter.70
  1619.2 79.1 reduce-scatter.68
  1702.5 79.0 reduce-scatter.66
  1785.7 79.1 reduce-scatter.64
  1868.9 79.0 reduce-scatter.62
  1952.0 79.1 reduce-scatter.60
  2068.2 68.2 reduce-scatter.42
  2140.1 66.5 reduce-scatter.40
  2210.2 66.7 reduce-scatter.46
  2280.5 66.7 reduce-scatter.44
  2350.8 78.6 reduce-scatter.58
  2433.1 78.8 reduce-scatter.56
  2515.5 79.1 reduce-scatter.50
  2598.2 79.1 reduce-scatter.48
  2680.9 79.1 reduce-scatter.54
  2763.6 79.0 reduce-scatter.52
  (16 shorter events, 421.0 us)
where the time goes:
time: 2860 us; the launch traced here: 2850 us
  waiting for transfers between devices  2450 us (86%)
  matrix products  240 us (8%)
  other arithmetic  56.9 us (2%)
  local copies, waits for them, and re-layouts  49.2 us (2%)
  blocking collectives  41 us (1%)
    reduce_scatter x16, waiting for transfers between devices, local(): lax.psum_scatter(shortened(attn_grads + (output_grad_t, gelu_grad, up_gra...  1120 us
    all_gather x12, waiting for transfers between devices, fold_rows(): lax.all_gather(a, 'dp', axis=0, tiled=True)  684 us
    all_gather x4, waiting for transfers between devices, map_columns(): lax.all_gather(weight, 'dp', axis=1, tiled=True)  254 us
    reduce_scatter x8, waiting for transfers between devices, sum_rows(): lax.psum_scatter(part.astype(jnp.bfloat16), 'tensor', scatter_dimension=0...  234 us
    all_gather x8, waiting for transfers between devices, gather_rows(): return lax.all_gather(rows, 'tensor', axis=0, tiled=True)  152 us
    dot_general x12, matrix products, fold_rows(): jnp.dot(acts, p, preferred_element_type=jnp.float32)  63.3 us
  transfers between devices with their start and end apart: 48, of which 46 were waited for; matrix products, arithmetic and copies ran while one was open for 8% of the time, Pallas kernels for 0%

commit v1 on v0

--- a/solution.py
+++ b/solution.py
@@ -1,15 +1,830 @@
+import functools
+
 import jax
 import jax.numpy as jnp
 from jax import lax
+from jax.experimental import pallas as pl
+from jax.experimental.pallas import tpu as pltpu
 from jax.sharding import PartitionSpec as P
 
 HEAD_QK = 256
 HEAD_V = 432
 LEN = 512
 
-
 EPS = 1e-06
 HEAD_FLOOR = 1.0
+NN = (((1,), (0,)), ((), ()))
+NT = (((1,), (1,)), ((), ()))
+TN = (((0,), (0,)), ((), ()))
+MESH = pl.DeviceIdType.MESH
+BF16 = jnp.bfloat16
+F32 = jnp.float32
+LOOK = 3
+VMEM_LIMIT = 60 * 1024 * 1024
+
+
+def dot(a, b, dims=NN):
+    return lax.dot_general(a, b, dims, preferred_element_type=F32)
+
+
+def loop(steps, body):
+    lax.fori_loop(0, steps, lambda i, c: (body(i), c)[1], 0)
+
+
+class Place:
+    def __init__(self):
+        dp, tensor = lax.axis_index("dp"), lax.axis_index("tensor")
+        self.dp, self.tensor = dp, tensor
+        self.z, self.y = lax.div(dp, 2), lax.rem(dp, 2)
+        self.x, self.c = lax.div(tensor, 2), lax.rem(tensor, 2)
+        self.half = lax.rem(self.z, 2)
+        self.zn = self.z + 1 - 2 * self.half
+
+    def at(self, z=None, y=None, x=None, c=None):
+        z = self.z if z is None else z
+        y = self.y if y is None else y
+        x = self.x if x is None else x
+        c = self.c if c is None else c
+        return (z * 2 + y, x * 2 + c)
+
+    def zplus(self, d):
+        return lax.rem(self.z + d + 4, 4)
+
+    def sib(self):
+        return self.at(c=1 - self.c)
+
+    def xn(self):
+        return self.at(x=1 - self.x)
+
+    def yn(self):
+        return self.at(y=1 - self.y)
+
+    def znb(self):
+        return self.at(z=self.zn)
+
+    def peers(self):
+        return [self.sib(), self.xn(), self.yn()] + [self.at(z=self.zplus(d)) for d in (1, 2, 3)]
+
+    def greet(self):
+        bar = pltpu.get_barrier_semaphore()
+        peers = self.peers()
+        for p in peers:
+            pl.semaphore_signal(bar, inc=1, device_id=p, device_id_type=MESH)
+        pl.semaphore_wait(bar, len(peers))
+
+
+def remote(src, dst, ssem, rsem, dev):
+    return pltpu.make_async_remote_copy(
+        src_ref=src, dst_ref=dst, send_sem=ssem, recv_sem=rsem, device_id=dev, device_id_type=MESH
+    )
+
+
+def block(half, tensor, rows):
+    return pl.ds(pl.multiple_of((half * 4 + tensor) * rows, rows), rows)
+
+
+def gather_acts(me, buf, rows, ssem, rsem, fill=()):
+    fill = list(fill)
+
+    def step():
+        if fill:
+            fill.pop(0)()
+
+    def move(k, half, x, dev):
+        r = block(half, x * 2 + me.c, rows)
+        return remote(buf.at[r], buf.at[r], ssem.at[k], rsem.at[k], dev)
+
+    h, x = me.half, me.x
+    own_x = move(0, h, x, me.xn())
+    own_z = move(1, h, x, me.znb())
+    own_s = move(2, h, x, me.sib())
+    own_x.start()
+    own_z.start()
+    own_s.start()
+    step()
+    own_z.wait_recv()
+    z_x = move(3, 1 - h, x, me.xn())
+    z_s = move(4, 1 - h, x, me.sib())
+    z_x.start()
+    z_s.start()
+    own_x.wait_recv()
+    x_s = move(5, h, 1 - x, me.sib())
+    x_s.start()
+    step()
+    z_x.wait_recv()
+    g_s = move(6, 1 - h, 1 - x, me.sib())
+    g_s.start()
+    for m in (own_s, z_s, x_s, g_s):
+        m.wait_recv()
+    for m in (own_x, own_z, own_s, z_x, z_s, x_s, g_s):
+        m.wait_send()
+    while fill:
+        step()
+
+
+def sum_acts(me, part, rows, sib_buf, x_buf, z_buf, ssem, rsem, body, fill=()):
+    fill = list(fill)
+
+    def step():
+        if fill:
+            fill.pop(0)()
+
+    h, x = me.half, me.x
+    order = [(1 - h, 1 - x), (h, 1 - x), (1 - h, x), (h, x)]
+    sibs = []
+    for j, (hh, xx) in enumerate(order):
+        m = remote(part.at[block(hh, xx * 2 + 1 - me.c, rows)], sib_buf.at[j], ssem.at[j], rsem.at[j], me.sib())
+        m.start()
+        sibs.append(m)
+    chunk = 64
+
+    def mine(j, i):
+        hh, xx = order[j]
+        return pl.ds(pl.multiple_of((hh * 4 + xx * 2 + me.c) * rows + i * chunk, chunk), chunk)
+
+    def add(j, extra=None):
+        def go(i):
+            r = mine(j, i)
+            k = pl.ds(pl.multiple_of(i * chunk, chunk), chunk)
+            v = part[r, :].astype(F32) + sib_buf[j, k, :].astype(F32)
+            if extra is not None:
+                v = v + extra[k, :].astype(F32)
+            part[r, :] = v.astype(BF16)
+
+        loop(rows // chunk, go)
+
+    def my_block(j):
+        hh, xx = order[j]
+        return part.at[block(hh, xx * 2 + me.c, rows)]
+
+    to_x = []
+    for j in (0, 1):
+        sibs[j].wait_recv()
+        add(j)
+        m = remote(my_block(j), x_buf.at[j], ssem.at[4 + j], rsem.at[4 + j], me.xn())
+        m.start()
+        to_x.append(m)
+    step()
+    sibs[2].wait_recv()
+    to_x[0].wait_recv()
+    add(2, x_buf.at[0])
+    to_z = remote(my_block(2), z_buf, ssem.at[6], rsem.at[6], me.znb())
+    to_z.start()
+    sibs[3].wait_recv()
+    step()
+    to_x[1].wait_recv()
+    to_z.wait_recv()
+    small = 32
+
+    def last(i):
+        k = pl.ds(pl.multiple_of(i * small, small), small)
+        r = pl.ds(pl.multiple_of((h * 4 + x * 2 + me.c) * rows + i * small, small), small)
+        v = part[r, :].astype(F32) + sib_buf[3, k, :].astype(F32)
+        v = v + x_buf[1, k, :].astype(F32) + z_buf[k, :].astype(F32)
+        body(i * small, small, v)
+
+    loop(rows // small, last)
+    for m in sibs + to_x + [to_z]:
+        m.wait_send()
+    while fill:
+        step()
+
+
+def unit_rows(qk, val, ffn):
+    sizes = (("q", qk), ("k", qk), ("v", val), ("s", val), ("o", val), ("g", ffn), ("u", ffn), ("d", ffn))
+    out, at = {}, 0
+    for name, n in sizes:
+        out[name] = (at, n)
+        at += n
+    return out, at
+
+
+def rms(v, floor):
+    return lax.rsqrt(jnp.mean(v * v, -1, keepdims=True) + floor)
+
+
+def forward_kernel(
+    dims,
+    tokens, mask, cosine, sine, attn_gain, ffn_gain, wl,
+    output, x_mid, mids, wf, s_n, s_nf, s_q, s_k, s_v, s_s, s_m, s_gt, s_g, s_u, s_h, s_p,
+    W, N0, N1, part, sib_buf, x_buf, z_buf, q, k, v, s, m, gt, g, u, h, p,
+    zs, zr, ys, yr, lo, ld, ags, agr, rss, rsr, sv,
+):
+    layers, rows, lanes, units, scale = dims
+    me = Place()
+    names = list(units)
+    groups = [(l, units[n]) for l in range(layers) for n in names]
+    spot = {(l, n): l * len(names) + i for l in range(layers) for i, n in enumerate(names)}
+    my_lane = pl.multiple_of(me.dp * lanes, lanes)
+
+    def z_copy(i, d):
+        l, (r0, n) = groups[i]
+        tz = me.zplus(d)
+        return remote(
+            wl.at[l, lax.rem(tz, 2), pl.ds(r0, n)], wf.at[l, pl.ds(r0, n), pl.ds(my_lane, lanes)],
+            zs.at[i, d - 1], zr.at[i, d - 1], me.at(z=tz),
+        )
+
+    def y_copy(i, d):
+        l, (r0, n) = groups[i]
+        lane = pl.ds(pl.multiple_of((me.zplus(-d) * 2 + me.y) * lanes, lanes), lanes)
+        dst = wf.at[l, pl.ds(r0, n), lane]
+        src = wl.at[l, me.half, pl.ds(r0, n)] if d == 0 else dst
+        return remote(src, dst, ys.at[i, d], yr.at[i, d], me.yn())
+
+    def local_copy(i):
+        l, (r0, n) = groups[i]
+        return pltpu.make_async_copy(
+            wl.at[l, me.half, pl.ds(r0, n)], wf.at[l, pl.ds(r0, n), pl.ds(my_lane, lanes)], lo.at[i]
+        )
+
+    def issue(i):
+        if i < len(groups):
+            for d in (1, 2, 3):
+                z_copy(i, d).start()
+            y_copy(i, 0).start()
+            local_copy(i).start()
+
+    done = [0]
+
+    def advance():
+        i = done[0]
+        if i >= len(groups):
+            return
+        done[0] += 1
+        for d in (1, 3, 2):
+            z_copy(i, d).wait_recv()
+            y_copy(i, d).start()
+        issue(i + LOOK)
+
+    def take(l, *wanted):
+        idx = [spot[l, n] for n in wanted]
+        while done[0] <= min(idx[-1] + 1, len(groups) - 1):
+            advance()
+        copies = []
+        for i in idx:
+            for d in range(4):
+                y_copy(i, d).wait_recv()
+            local_copy(i).wait()
+            r0, n = groups[i][1]
+            c = pltpu.make_async_copy(wf.at[l, pl.ds(r0, n)], W.at[pl.ds(r0, n)], ld.at[i])
+            c.start()
+            copies.append(c)
+        for c in copies:
+            c.wait()
+
+    saves = []
+
+    def save(src, dst):
+        c = pltpu.make_async_copy(src, dst, sv.at[len(saves)])
+        c.start()
+        saves.append(c)
+
+    waited = [0]
+
+    def settle():
+        while waited[0] < len(saves):
+            saves[waited[0]].wait()
+            waited[0] += 1
+
+    def weight(n):
+        r0, size = units[n]
+        return W[pl.ds(r0, size), :]
+
+    def seq_rows(i):
+        return pl.ds(pl.multiple_of(i * LEN, LEN), LEN)
+
+    seqs = 2
+    own = (me.half * 4 + me.tensor) * rows
+
+    def own_rows(r0, n):
+        return pl.ds(pl.multiple_of(own + r0, n), n)
+
+    me.greet()
+    for i in range(LOOK):
+        issue(i)
+
+    small = 32
+
+    def first_norm(i):
+        r = pl.ds(pl.multiple_of(i * small, small), small)
+        x = tokens[r, :].astype(F32)
+        N0[own_rows(i * small, small), :] = (x * rms(x, EPS) * attn_gain[0:1, :]).astype(BF16)
+
+    loop(rows // small, first_norm)
+
+    for l in range(layers):
+        gather_acts(me, N0, rows, ags.at[2 * l], agr.at[2 * l], (advance,))
+        save(N0, s_n.at[l])
+        for name, dst in (("q", q), ("k", k)):
+            take(l, name)
+
+            def project(i, name=name, dst=dst):
+                r = seq_rows(i)
+                t = dot(N0[r, :], weight(name), NT)
+                half = t.shape[1] // 2
+                t1, t2 = t[:, :half], t[:, half:]
+                c, sn = cosine[...], sine[...]
+                dst[r, :half] = (t1 * c - t2 * sn).astype(BF16)
+                dst[r, half:] = (t2 * c + t1 * sn).astype(BF16)
+
+            loop(seqs, project)
+        save(q, s_q.at[l])
+        save(k, s_k.at[l])
+        take(l, "v")
+
+        def values(i):
+            r = seq_rows(i)
+            v[r, :] = dot(N0[r, :], weight("v"), NT).astype(BF16)
+
+        loop(seqs, values)
+        save(v, s_v.at[l])
+
+        def retain(i):
+            r = seq_rows(i)
+            raw = dot(q[r, :], k[r, :], NT) * scale
+            probs = (raw * mask[i]).astype(BF16)
+            p[i] = probs
+            m[r, :] = dot(probs, v[r, :])
+
+        loop(seqs, retain)
+        save(p, s_p.at[l])
+        save(m, s_m.at[l])
+        take(l, "s")
+
+        def gate(i):
+            r = seq_rows(i)
+            t = dot(N0[r, :], weight("s"), NT)
+            s[r, :] = t
+            mix = m[r, :]
+            gt[r, :] = (jax.nn.silu(t) * (mix * rms(mix, HEAD_FLOOR))).astype(BF16)
+
+        loop(seqs, gate)
+        save(s, s_s.at[l])
+        save(gt, s_gt.at[l])
+        take(l, "o")
+
+        def project_out(i, src=gt, name="o"):
+            r = pl.ds(pl.multiple_of(i * 256, 256), 256)
+            part[r, :] = dot(src[r, :], weight(name)).astype(BF16)
+
+        loop(seqs * LEN // 256, project_out)
+
+        def to_mid(r0, n, total, l=l):
+            r = pl.ds(pl.multiple_of(r0, n), n)
+            x = (tokens[r, :].astype(F32) if l == 0 else x_mid[l - 1, r, :]) + total
+            mids[l, r, :] = x
+            N1[own_rows(r0, n), :] = (x * rms(x, EPS) * ffn_gain[l : l + 1, :]).astype(BF16)
+
+        sum_acts(me, part, rows, sib_buf, x_buf, z_buf, rss.at[2 * l], rsr.at[2 * l], to_mid, (advance,))
+        gather_acts(me, N1, rows, ags.at[2 * l + 1], agr.at[2 * l + 1], (advance,))
+        save(N1, s_nf.at[l])
+        take(l, "g")
+
+        def gates(i):
+            r = seq_rows(i)
+            g[r, :] = dot(N1[r, :], weight("g"), NT)
+
+        loop(seqs, gates)
+        take(l, "u")
+
+        def ups(i):
+            r = seq_rows(i)
+            t = dot(N1[r, :], weight("u"), NT)
+            u[r, :] = t
+            h[r, :] = (jax.nn.gelu(g[r, :], approximate=True) * t).astype(BF16)
+
+        loop(seqs, ups)
+        save(g, s_g.at[l])
+        save(u, s_u.at[l])
+        save(h, s_h.at[l])
+        take(l, "d")
+        loop(seqs * LEN // 256, functools.partial(project_out, src=h, name="d"))
+
+        def to_next(r0, n, total, l=l):
+            r = pl.ds(pl.multiple_of(r0, n), n)
+            x = mids[l, r, :] + total
+            if l + 1 < layers:
+                x_mid[l, r, :] = x
+                N0[own_rows(r0, n), :] = (x * rms(x, EPS) * attn_gain[l + 1 : l + 2, :]).astype(BF16)
+            else:
+                output[r, :] = x.astype(BF16)
+
+        settle()
+        sum_acts(me, part, rows, sib_buf, x_buf, z_buf, rss.at[2 * l + 1], rsr.at[2 * l + 1], to_next, (advance,))
+    settle()
+    for i in range(len(groups)):
+        for d in (1, 2, 3):
+            z_copy(i, d).wait_send()
+        for d in range(4):
+            y_copy(i, d).wait_send()
+
+
+def run_forward(dims, tokens, mask, cosine, sine, attn_gain, ffn_gain, wl):
+    layers, rows, lanes, units, scale = dims
+    depth = tokens.shape[1]
+    total = wl.shape[2]
+    group = 8 * rows
+    seqs = group // LEN
+    qk, val, ffn = units["q"][1], units["v"][1], units["g"][1]
+    vm = pl.BlockSpec(memory_space=pltpu.VMEM)
+    hb = pl.BlockSpec(memory_space=pl.ANY)
+    outs = [
+        ((rows, depth), BF16), ((layers - 1, rows, depth), F32), ((layers, rows, depth), F32),
+        ((layers, total, depth), BF16), ((layers, group, depth), BF16), ((layers, group, depth), BF16),
+        ((layers, group, qk), BF16), ((layers, group, qk), BF16), ((layers, group, val), BF16),
+        ((layers, group, val), F32), ((layers, group, val), F32), ((layers, group, val), BF16),
+        ((layers, group, ffn), F32), ((layers, group, ffn), F32), ((layers, group, ffn), BF16),
+        ((layers, seqs, LEN, LEN), BF16),
+    ]
+    n_groups = layers * len(units)
+    dma = pltpu.SemaphoreType.DMA
+    return pl.pallas_call(
+        functools.partial(forward_kernel, dims),
+        out_shape=[jax.ShapeDtypeStruct(s, d) for s, d in outs],
+        in_specs=[vm] * 6 + [hb],
+        out_specs=[vm] * 3 + [hb] * 13,
+        scratch_shapes=[
+            pltpu.VMEM((total, depth), BF16),
+            pltpu.VMEM((group, depth), BF16), pltpu.VMEM((group, depth), BF16), pltpu.VMEM((group, depth), BF16),
+            pltpu.VMEM((4, rows, depth), BF16), pltpu.VMEM((2, rows, depth), BF16), pltpu.VMEM((rows, depth), BF16),
+            pltpu.VMEM((group, qk), BF16), pltpu.VMEM((group, qk), BF16), pltpu.VMEM((group, val), BF16),
+            pltpu.VMEM((group, val), F32), pltpu.VMEM((group, val), F32), pltpu.VMEM((group, val), BF16),
+            pltpu.VMEM((group, ffn), F32), pltpu.VMEM((group, ffn), F32), pltpu.VMEM((group, ffn), BF16),
+            pltpu.VMEM((seqs, LEN, LEN), BF16),
+            dma((n_groups, 3)), dma((n_groups, 3)), dma((n_groups, 4)), dma((n_groups, 4)),
+            dma((n_groups,)), dma((n_groups,)),
+            dma((2 * layers, 7)), dma((2 * layers, 7)), dma((2 * layers, 7)), dma((2 * layers, 7)),
+            dma((12 * layers,)),
+        ],
+        compiler_params=pltpu.CompilerParams(collective_id=0, has_side_effects=True, vmem_limit_bytes=VMEM_LIMIT),
+    )(tokens, mask, cosine, sine, attn_gain, ffn_gain, wl)
+
+
+SLOTS = 4
+
+
+def backward_kernel(
+    dims,
+    cot, tokens, x_mid, mids, mask, cosine, sine, attn_gain, ffn_gain,
+    wf, s_n, s_nf, s_q, s_k, s_v, s_s, s_m, s_gt, s_g, s_u, s_h, s_p,
+    input_grad, gains, rz,
+    gr, nb, ga0, ga1, part, sib_buf, x_buf, z_buf, W, a1, a2, a3, q, k, v, p, t1, t2, tq, tk, G, ry, acc, acc_in,
+    ys, yr, zs, zr, os, ags, agr, rss, rsr, ld, gns, gnr, credit,
+):
+    layers, rows, lanes, units, scale = dims
+    me = Place()
+    depth = cot.shape[1]
+    wide = 512
+    small = 32
+    seqs = 2
+    order = list(reversed(range(layers)))
+    jobs = [(l, n) for l in order for n in ("d", "g", "u", "o", "q", "k", "v", "s")]
+    index = {job: i for i, job in enumerate(jobs)}
+    own = (me.half * 4 + me.tensor) * rows
+    ffn_row = units["g"][0]
+    attn_end = ffn_row
+    total_rows = units["d"][0] + units["d"][1]
+
+    def own_rows(r0, n):
+        return pl.ds(pl.multiple_of(own + r0, n), n)
+
+    def seq_rows(i):
+        return pl.ds(pl.multiple_of(i * LEN, LEN), LEN)
+
+    def lane(i):
+        return pl.ds(pl.multiple_of(i * lanes, lanes), lanes)
+
+    def y_send(i, d):
+        n = units[jobs[i][1]][1]
+        tz = me.zplus(d)
+        return remote(
+            G.at[i % SLOTS, pl.ds(0, n), lane(tz * 2 + 1 - me.y)], ry.at[i % SLOTS, pl.ds(0, n), lane(tz)],
+            ys.at[i, d], yr.at[i, d], me.yn(),
+        )
+
+    def z_send(i, d):
+        l, name = jobs[i]
+        r0, n = units[name]
+        tz = me.zplus(d)
+        return remote(
+            G.at[i % SLOTS, pl.ds(0, n), lane(tz * 2 + me.y)], rz.at[l, me.half, d // 2, pl.ds(r0, n)],
+            zs.at[i, d - 1], zr.at[i, d - 1], me.at(z=tz),
+        )
+
+    def own_copy(i):
+        l, name = jobs[i]
+        r0, n = units[name]
+        return pltpu.make_async_copy(
+            G.at[i % SLOTS, pl.ds(0, n), lane(me.dp)], rz.at[l, me.half, 0, pl.ds(r0, n)], os.at[i]
+        )
+
+    def retire(i):
+        for d in range(4):
+            y_send(i, d).wait_send()
+        for d in (1, 2, 3):
+            z_send(i, d).wait_send()
+        own_copy(i).wait()
+
+    def make(l, name, left, right):
+        i = index[l, name]
+        n = units[name][1]
+        if i >= SLOTS:
+            retire(i - SLOTS)
+
+        def go(j):
+            cols = pl.ds(pl.multiple_of(j * wide, wide), wide)
+            G[i % SLOTS, :n, cols] = dot(left[...], right[:, cols], TN).astype(BF16)
+
+        loop(depth // wide, go)
+        if i >= SLOTS:
+            pl.semaphore_wait(credit.at[i % SLOTS], 1)
+        for d in (2, 1, 3, 0):
+            y_send(i, d).start()
+
+    def combine(l, name):
+        i = index[l, name]
+        n = units[name][1]
+        for d in (2, 1, 3, 0):
+            y_send(i, d).wait_recv()
+            tz = me.zplus(d)
+
+            def add(j, tz=tz):
+                r = pl.ds(pl.multiple_of(j * 16, 16), 16)
+                c = lane(tz * 2 + me.y)
+                both = G[i % SLOTS, r, c].astype(F32) + ry[i % SLOTS, r, lane(tz)].astype(F32)
+                G[i % SLOTS, r, c] = both.astype(BF16)
+
+            loop(n // 16, add)
+            if d:
+                z_send(i, d).start()
+            else:
+                own_copy(i).start()
+        if i + SLOTS < len(jobs):
+            pl.semaphore_signal(credit.at[i % SLOTS], inc=1, device_id=me.yn(), device_id_type=MESH)
+
+    spots = {}
+
+    def load(key, src, dst):
+        c = pltpu.make_async_copy(src, dst, ld.at[len(spots)])
+        c.start()
+        spots[key] = c
+
+    def ready(*keys):
+        for key in keys:
+            spots[key].wait()
+
+    def load_ffn(l):
+        load(("wf", l), wf.at[l, pl.ds(ffn_row, total_rows - ffn_row)], W.at[pl.ds(0, total_rows - ffn_row)])
+        load(("g", l), s_g.at[l], a1)
+        load(("u", l), s_u.at[l], a2)
+
+    def load_attn(l):
+        load(("wa", l), wf.at[l, pl.ds(0, attn_end)], W.at[pl.ds(0, attn_end)])
+        load(("s", l), s_s.at[l], a1)
+        load(("m", l), s_m.at[l], a2)
+        load(("q", l), s_q.at[l], q)
+        load(("k", l), s_k.at[l], k)
+        load(("v", l), s_v.at[l], v)
+        load(("p", l), s_p.at[l], p)
+
+    def load_h(l):
+        load(("h", l), s_h.at[l], a3)
+
+    def load_nf(l):
+        load(("nf", l), s_nf.at[l], nb)
+
+    def load_gt(l):
+        load(("gt", l), s_gt.at[l], a3)
+
+    def load_n(l):
+        load(("n", l), s_n.at[l], nb)
+
+    def weight(name, base):
+        r0, n = units[name]
+        return W[pl.ds(r0 - base, n), :]
+
+    def norm_back(x, gain, dn, gain_row):
+        e = rms(x, EPS)
+        gx = dn * gain
+        inner = jnp.sum(gx * x, -1, keepdims=True)
+        acc[0, gain_row : gain_row + 1, :] += jnp.sum(dn * x * e, 0, keepdims=True)
+        return e * gx - (e * e * e) * x * (inner / depth)
+
+    me.greet()
+    load_ffn(order[0])
+    load_h(order[0])
+    load_nf(order[0])
+    acc[0] = jnp.zeros(acc.shape[1:], F32)
+
+    def begin(i):
+        r = pl.ds(pl.multiple_of(i * small, small), small)
+        gr[r, :] = cot[r, :].astype(F32)
+        ga0[own_rows(i * small, small), :] = cot[r, :]
+
+    loop(rows // small, begin)
+    later = []
+    for at, l in enumerate(order):
+        last = at == layers - 1
+        gather_acts(me, ga0, rows, ags.at[2 * at], agr.at[2 * at], later)
+        ready(("wf", l), ("g", l), ("u", l))
+
+        def ffn_back(i):
+            r = seq_rows(i)
+            gh = dot(ga0[r, :], weight("d", ffn_row), NT)
+            g, u = a1[r, :], a2[r, :]
+            th = jnp.tanh(0.7978845608028654 * (g + 0.044715 * g * g * g))
+            val = 0.5 * g * (1.0 + th)
+            slope = 0.5 * (1.0 + th) + 0.5 * g * (1.0 - th * th) * (0.7978845608028654 * (1.0 + 0.134145 * g * g))
+            t1[r, :] = (gh * u * slope).astype(BF16)
+            t2[r, :] = (gh * val).astype(BF16)
+
+        loop(seqs, ffn_back)
+
+        def ffn_sum(i):
+            r = pl.ds(pl.multiple_of(i * 256, 256), 256)
+            part[r, :] = (dot(t1[r, :], weight("g", ffn_row)) + dot(t2[r, :], weight("u", ffn_row))).astype(BF16)
+
+        loop(seqs * LEN // 256, ffn_sum)
+        load_attn(l)
+        ready(("h", l), ("nf", l))
+
+        def fill_d(l=l):
+            make(l, "d", a3, ga0)
+            load_gt(l)
+
+        def fill_gu(l=l):
+            make(l, "g", t1, nb)
+            make(l, "u", t2, nb)
+            load_n(l)
+
+        def to_mid(r0, n, tot, l=l):
+            r = pl.ds(pl.multiple_of(r0, n), n)
+            new = gr[r, :] + norm_back(mids[l, r, :], ffn_gain[l : l + 1, :], tot, layers + l)
+            gr[r, :] = new
+            ga1[own_rows(r0, n), :] = new.astype(BF16)
+
+        sum_acts(me, part, rows, sib_buf, x_buf, z_buf, rss.at[2 * at], rsr.at[2 * at], to_mid, (fill_d, fill_gu))
+        mids_of = functools.partial
+        gather_acts(
+            me, ga1, rows, ags.at[2 * at + 1], agr.at[2 * at + 1],
+            (mids_of(combine, l, "d"), mids_of(combine, l, "g")),
+        )
+        ready(("wa", l), ("s", l), ("m", l), ("q", l), ("k", l), ("v", l), ("p", l))
+
+        def attn_back(i):
+            r = seq_rows(i)
+            gg = dot(ga1[r, :], weight("o", 0), NT)
+            s, mix = a1[r, :], a2[r, :]
+            sig = 1.0 / (1.0 + jnp.exp(-s))
+            rr = rms(mix, HEAD_FLOOR)
+            t2[r, :] = (gg * (mix * rr) * (sig * (1.0 + s * (1.0 - sig)))).astype(BF16)
+            gz = gg * (s * sig)
+            inner = jnp.sum(gz * mix, -1, keepdims=True) / mix.shape[1]
+            gm = (rr * gz - (rr * rr * rr) * mix * inner).astype(BF16)
+            raw = (dot(gm, v[r, :], NT) * mask[i]).astype(BF16)
+            t1[r, :] = dot(p[i], gm, TN).astype(BF16)
+            c, sn = cosine[...], sine[...]
+            for dst, grad in ((tq, dot(raw, k[r, :]) * scale), (tk, dot(raw, q[r, :], TN) * scale)):
+                half = grad.shape[1] // 2
+                g1, g2 = grad[:, :half], grad[:, half:]
+                dst[r, :half] = (g1 * c + g2 * sn).astype(BF16)
+                dst[r, half:] = (g2 * c - g1 * sn).astype(BF16)
+
+        loop(seqs, attn_back)
+
+        def attn_sum(i):
+            r = pl.ds(pl.multiple_of(i * 256, 256), 256)
+            tot = dot(tq[r, :], weight("q", 0)) + dot(tk[r, :], weight("k", 0))
+            tot = tot + dot(t1[r, :], weight("v", 0)) + dot(t2[r, :], weight("s", 0))
+            part[r, :] = tot.astype(BF16)
+
+        loop(seqs * LEN // 256, attn_sum)
+        if not last:
+            load_ffn(order[at + 1])
+        ready(("gt", l), ("n", l))
+
+        def fill_o(l=l):
+            combine(l, "u")
+            make(l, "o", a3, ga1)
+            make(l, "q", tq, nb)
+
+        def fill_kv(l=l, last=last):
+            combine(l, "o")
+            make(l, "k", tk, nb)
+            combine(l, "q")
+            make(l, "v", t1, nb)
+            make(l, "s", t2, nb)
+            if not last:
+                load_nf(l - 1)
+                load_h(l - 1)
+
+        def to_prev(r0, n, tot, l=l, last=last):
+            r = pl.ds(pl.multiple_of(r0, n), n)
+            x = tokens[r, :].astype(F32) if l == 0 else x_mid[l - 1, r, :]
+            new = gr[r, :] + norm_back(x, attn_gain[l : l + 1, :], tot, l)
+            if last:
+                input_grad[r, :] = new
+            else:
+                gr[r, :] = new
+                ga0[own_rows(r0, n), :] = new.astype(BF16)
+
+        sum_acts(me, part, rows, sib_buf, x_buf, z_buf, rss.at[2 * at + 1], rsr.at[2 * at + 1], to_prev, (fill_o, fill_kv))
+        later = [mids_of(combine, l, "k"), mids_of(combine, l, "v"), mids_of(combine, l, "s")]
+
+    for go in later:
+        go()
+    partners = [me.sib(), me.xn(), me.yn(), me.znb(), me.at(z=me.zplus(2))]
+    for j, dev in enumerate(partners):
+        m = remote(acc.at[j], acc_in.at[j], gns.at[j], gnr.at[j], dev)
+        m.start()
+        m.wait()
+        acc[j + 1] = acc[j] + acc_in[j]
+    gains[...] = acc[len(partners)]
+    for i in range(len(jobs) - SLOTS, len(jobs)):
+        retire(i)
+    for i in range(len(jobs)):
+        for d in (1, 2, 3):
+            z_send(i, d).wait_recv()
+
+
+def run_backward(dims, cot, tokens, x_mid, mids, mask, cosine, sine, attn_gain, ffn_gain, kept):
+    layers, rows, lanes, units, scale = dims
+    depth = tokens.shape[1]
+    total = kept[0].shape[1]
+    group = 8 * rows
+    seqs = group // LEN
+    qk, val, ffn = units["q"][1], units["v"][1], units["g"][1]
+    vm = pl.BlockSpec(memory_space=pltpu.VMEM)
+    hb = pl.BlockSpec(memory_space=pl.ANY)
+    outs = [((rows, depth), F32), ((8, depth), F32), ((layers, 2, 2, total, lanes), BF16)]
+    jobs = layers * len(units)
+    most = max(n for _, n in units.values())
+    attn_rows = units["g"][0]
+    dma = pltpu.SemaphoreType.DMA
+    big = pltpu.VMEM((group, depth), BF16)
+    return pl.pallas_call(
+        functools.partial(backward_kernel, dims),
+        out_shape=[jax.ShapeDtypeStruct(s, d) for s, d in outs],
+        in_specs=[vm] * 9 + [hb] * 13,
+        out_specs=[vm] * 2 + [hb],
+        scratch_shapes=[
+            pltpu.VMEM((rows, depth), F32), big, big, big, big,
+            pltpu.VMEM((4, rows, depth), BF16), pltpu.VMEM((2, rows, depth), BF16), pltpu.VMEM((rows, depth), BF16),
+            pltpu.VMEM((max(attn_rows, total - attn_rows), depth), BF16),
+            pltpu.VMEM((group, val), F32), pltpu.VMEM((group, val), F32), pltpu.VMEM((group, val), BF16),
+            pltpu.VMEM((group, qk), BF16), pltpu.VMEM((group, qk), BF16), pltpu.VMEM((group, val), BF16),
+            pltpu.VMEM((seqs, LEN, LEN), BF16),
+            pltpu.VMEM((group, val), BF16), pltpu.VMEM((group, val), BF16),
+            pltpu.VMEM((group, qk), BF16), pltpu.VMEM((group, qk), BF16),
+            pltpu.VMEM((SLOTS, most, depth), BF16), pltpu.VMEM((SLOTS, most, depth // 2), BF16),
+            pltpu.VMEM((6, 8, depth), F32), pltpu.VMEM((5, 8, depth), F32),
+            dma((jobs, 4)), dma((jobs, 4)), dma((jobs, 3)), dma((jobs, 3)), dma((jobs,)),
+            dma((2 * layers, 7)), dma((2 * layers, 7)), dma((2 * layers, 7)), dma((2 * layers, 7)),
+            dma((16 * layers,)), dma((5,)), dma((5,)), pltpu.SemaphoreType.REGULAR((SLOTS,)),
+        ],
+        compiler_params=pltpu.CompilerParams(collective_id=1, has_side_effects=True, vmem_limit_bytes=VMEM_LIMIT),
+    )(cot, tokens, x_mid, mids, mask, cosine, sine, attn_gain, ffn_gain, *kept)
+
+def rotation(length, width):
+    half = width // 2
+    place = jnp.arange(length, dtype=F32)
+    freqs = 10000.0 ** (-jnp.arange(half, dtype=F32) / half)
+    angle = place[:, None] * freqs[None, :]
+    return jnp.cos(angle), jnp.sin(angle)
+
+
+def decay_mask(seg_rows, head, length):
+    place = jnp.arange(length, dtype=jnp.int32)
+    dist = place[:, None] - place[None, :]
+    same = (seg_rows[:, :, None] == seg_rows[:, None, :]) & (dist >= 0)[None]
+    rate = jnp.log1p(-(2.0 ** (-5.0 - head)))
+    decay = jnp.exp(jnp.maximum(dist, 0).astype(F32) * rate)
+    return jnp.where(same, decay[None], 0.0)
+
+
+def stack_weights(w_query, w_key, w_value, w_swish, w_output, w_gelu, w_up, w_down):
+    def cut(w):
+        return w.reshape(w.shape[0], 2, w.shape[1] // 2, w.shape[2])
+
+    def turn(w):
+        return cut(jnp.swapaxes(w, 1, 2))
+
+    parts = [turn(w_query), turn(w_key), turn(w_value), turn(w_swish), cut(w_output), turn(w_gelu), turn(w_up), cut(w_down)]
+    return jnp.concatenate(parts, axis=2)
+
+
+def setup(segments, w_query, w_value, w_gelu):
+    dp, tensor = lax.axis_index("dp"), lax.axis_index("tensor")
+    half = (dp // 2) % 2
+    other = lax.ppermute(segments, "dp", [(i, i ^ 2) for i in range(8)])
+    pair = jnp.where(half == 0, jnp.stack([segments, other]), jnp.stack([other, segments]))
+    mask = decay_mask(pair, (tensor * 2 + half).astype(F32), LEN)
+    cosine, sine = rotation(LEN, HEAD_QK)
+    units, total = unit_rows(w_query.shape[2] // 2, w_value.shape[2] // 2, w_gelu.shape[2] // 2)
+    return mask, cosine, sine, units
+
+
 CONTRACT_ROWS = (((0,), (0,)), ((), ()))
 CONTRACT_COLS = (((1,), (1,)), ((), ()))
 
@@ -30,7 +845,7 @@
     return jax.nn.gelu(values, approximate=True)
 
 
-def rotation(length, width):
+def plain_rotation(length, width):
     half = width // 2
     place = jnp.arange(length, dtype=jnp.float32)
     freqs = 10000.0 ** (-jnp.arange(half, dtype=jnp.float32) / half)
@@ -52,7 +867,7 @@
     return jnp.concatenate([first * cosine + second * sine, second * cosine - first * sine], -1)
 
 
-def decay_mask(seg_rows, head_ids, length):
+def plain_mask(seg_rows, head_ids, length):
     place = jnp.arange(length, dtype=jnp.int32)
     dist = place[:, None] - place[None, :]
     same = (seg_rows[:, :, None] == seg_rows[:, None, :]) & (dist >= 0)[None]
@@ -111,7 +926,7 @@
     )
 
 
-def local(
+def plain(
     tokens,
     segments,
     attn_gain,
@@ -131,8 +946,8 @@
     seqs = segments.shape[0] // LEN
     score_scale = HEAD_QK ** (-0.5)
     head_ids = (lax.axis_index("tensor") * heads_dev + jnp.arange(heads_dev)).astype(jnp.float32)
-    mask = decay_mask(segments.reshape(seqs, LEN), head_ids, LEN)
-    cosine, sine = rotation(LEN, HEAD_QK)
+    mask = plain_mask(segments.reshape(seqs, LEN), head_ids, LEN)
+    cosine, sine = plain_rotation(LEN, HEAD_QK)
     residual = tokens.astype(jnp.float32)
     saved = []
     for layer in range(layers):
@@ -303,34 +1118,37 @@
     )
 
 
+def grouped(
+    tokens, segments, attn_gain, w_query, w_key, w_value, w_swish, w_output, ffn_gain, w_gelu, w_up, w_down, cotangent
+):
+    layers = w_query.shape[0]
+    mask, cosine, sine, units = setup(segments, w_query, w_value, w_gelu)
+    wl = stack_weights(w_query, w_key, w_value, w_swish, w_output, w_gelu, w_up, w_down)
+    dims = (layers, tokens.shape[0], w_query.shape[1], units, HEAD_QK ** (-0.5))
+    output, x_mid, mids, *kept = run_forward(dims, tokens, mask, cosine, sine, attn_gain, ffn_gain, wl)
+    input_grad, gains, rz = run_backward(
+        dims, cotangent, tokens, x_mid, mids, mask, cosine, sine, attn_gain, ffn_gain, kept
+    )
+    sums = rz[:, :, 0].astype(F32) + rz[:, :, 1].astype(F32)
+
+    def piece(name):
+        r0, n = units[name]
+        part = sums[:, :, r0 : r0 + n]
+        return part.reshape(layers, 2 * n, part.shape[3])
+
+    def turned(name):
+        return jnp.swapaxes(piece(name), 1, 2)
+
+    return (
+        output, input_grad, gains[:layers], turned("q"), turned("k"), turned("v"), turned("s"), piece("o"),
+        gains[layers : 2 * layers], turned("g"), turned("u"), piece("d"),
+    )
+
+
 def solution(mesh):
-    in_specs = (
-        P(("dp", "tensor"), None),
-        P("dp"),
-        P(),
-        P(None, "dp", "tensor"),
-        P(None, "dp", "tensor"),
-        P(None, "dp", "tensor"),
-        P(None, "dp", "tensor"),
-        P(None, "tensor", "dp"),
-        P(),
-        P(None, "dp", "tensor"),
-        P(None, "dp", "tensor"),
-        P(None, "tensor", "dp"),
-        P(("dp", "tensor"), None),
-    )
-    out_specs = (
-        P(("dp", "tensor"), None),
-        P(("dp", "tensor"), None),
-        P(),
-        P(None, "dp", "tensor"),
-        P(None, "dp", "tensor"),
-        P(None, "dp", "tensor"),
-        P(None, "dp", "tensor"),
-        P(None, "tensor", "dp"),
-        P(),
-        P(None, "dp", "tensor"),
-        P(None, "dp", "tensor"),
-        P(None, "tensor", "dp"),
-    )
-    return jax.shard_map(local, mesh=mesh, in_specs=in_specs, out_specs=out_specs, check_vma=False)
+    rows = P(("dp", "tensor"), None)
+    up, down = P(None, "dp", "tensor"), P(None, "tensor", "dp")
+    in_specs = (rows, P("dp"), P(), up, up, up, up, down, P(), up, up, down, rows)
+    out_specs = (rows, rows, P(), up, up, up, up, down, P(), up, up, down)
+    step = grouped if (mesh.shape["dp"], mesh.shape["tensor"]) == (8, 4) else plain
+    return jax.shard_map(step, mesh=mesh, in_specs=in_specs, out_specs=out_specs, check_vma=False)

time: 2860 us -> 897 us (0.31)
  waiting for transfers between devices: 2450 us -> 0.01 us
  Pallas kernels: 0 us -> 840 us
  matrix products: 240 us -> 0 us
  other arithmetic: 56.9 us -> 14.3 us
  blocking collectives: 41 us -> 0 us
    reduce_scatter x24 -> x0, waiting for transfers between devices: 1350 us -> none  [the longest x16 1120 us: local(): lax.psum_scatter(shortened(attn_grads + (output_grad_t, gelu_grad, up_gra...]
    all_gather x24 -> x0, waiting for transfers between devices: 1090 us -> none  [the longest x12 684 us: fold_rows(): lax.all_gather(a, 'dp', axis=0, tiled=True)]
    pallas_call x0 -> x2, Pallas kernels: none -> 840 us  [the longest x1 439 us: run_forward(): pl.pallas_call(functools.partial(forward_kernel, dims), out_shape=[jax.Sh...]
    dot_general x60 -> x0, matrix products: 240 us -> none  [the longest x12 63.3 us: fold_rows(): jnp.dot(acts, p, preferred_element_type=jnp.float32)]
    psum x1 -> x0, blocking collectives: 41 us -> none  [local(): lax.psum((jnp.stack(attn_gain_parts), jnp.stack(ffn_gain_parts)), ('dp',...]
  transfers between devices with their start and end apart: 48 -> 1, of which waited for: 46 -> 0; matrix products, arithmetic and copies ran while one was open for 8% -> 2% of each run, Pallas kernels for 0% -> 0%
where the time goes in v1:
time: 897 us; the launch traced here: 888 us
  Pallas kernels  840 us (94%)
  local copies, waits for them, and re-layouts  28.7 us (3%)
  other arithmetic  14.3 us (2%)
    pallas_call x1, Pallas kernels, run_forward(): pl.pallas_call(functools.partial(forward_kernel, dims), out_shape=[jax.Sh...  439 us
    pallas_call x1, Pallas kernels, run_backward(): pl.pallas_call(functools.partial(backward_kernel, dims), out_shape=[jax.S...  401 us
  transfers between devices with their start and end apart: 1, of which 0 were waited for; matrix products, arithmetic and copies ran while one was open for 2% of the time, Pallas kernels for 0%

profile of v1, /device:TPU:0, one launch (start us, length us, event | category | flops | bytes accessed | tf_op | source)
XLA Modules:
  0.0 887.6 jit_solution(4892277771361308399)
XLA Ops:
  0.7 3.1 collective-permute-start
  3.8 1.7 fusion.1
  5.6 1.2 copy.25
  6.8 1.2 copy.26
  8.1 0.0 copy-start.2
  8.1 0.0 copy-start.3
  8.1 0.0 copy-start.4
  8.1 0.2 multiply_exponential_fusion
  8.3 0.0 copy-start.6
  8.3 0.9 constant_dynamic-update-slice_fusion.7
  9.2 0.8 constant_dynamic-update-slice_fusion.6
  10.0 1.0 constant_dynamic-update-slice_fusion.5
  11.0 2.2 constant_dynamic-update-slice_fusion.4
  13.2 0.0 copy-done.2
  13.2 1.0 constant_dynamic-update-slice_fusion.3
  14.2 1.0 constant_dynamic-update-slice_fusion.2
  15.2 2.1 constant_dynamic-update-slice_fusion.1
  17.3 1.0 constant_dynamic-update-slice_fusion.wl
  18.3 0.1 fusion
  18.4 0.0 collective-permute-done
  18.4 0.0 copy-done.6
  18.4 1.8 and_select_fusion.mask
  20.2 439.1 %shard_map.220 = (bf16[128,2048]{1,0:T(8,128)(2,1)}, f32[1,128,2048]{2,1,0:T(8,128)}, f32[2,128,2048]{2,1,0:T(8,128)}, bf16[2,3104,2048]{2,1,0:T(8,128)(2,1)}, b...) custom-call(bf16[128,2048]{1,0:T(8,128)(2,1)} %tokens.3, ...), custom_call_target="tpu_custom_call" | custom-call | tf_op jit(solution)/shard_map/pallas_call | solution.py:442
  459.3 401.1 %shard_map.221 = (f32[128,2048]{1,0:T(8,128)}, f32[8,2048]{1,0:T(8,128)}, bf16[2,2,2,3104,256]{4,3,2,1,0:T(8,128)(2,1)}) custom-call(bf16[128,2048]{1,0:T(8,128)(2,1)} %cot.1, bf16[128,2048]{1,0:T(8,128)(2,1)} %tokens.3, f32[1,128,2048]{2,1,0:T(8,128)} %get-tuple-element.32.x_mid, f32[2,128,2048]{2,1,0:T(8,128)} %get-tuple-element.33.mids, ...), custom_call_target="tpu_custom_call" | custom-call | tf_op jit(solution)/shard_map/pallas_call | solution.py:766
  860.5 10.5 %add_bitcast_fusion = f32[2,2,3104,256]{3,2,1,0:T(8,128)} fusion(bf16[2,2,2,3104,256]{4,3,2,1,0:T(8,128)(2,1)} %get-tuple-element.49), kind=kLoop, calls=%fused_computation | loop fusion | flops 9535488 | bytes 25427968 | tf_op jit(solution)/shard_map/add | solution.py:1132
  870.9 1.8 fusion.4
  872.7 8.3 fusion.3
  881.0 0.6 fusion.5
  881.6 1.3 copy.28
  883.0 1.3 copy.27
  884.3 1.9 copy.38
  886.1 1.0 copy.39
  (10 shorter events, 0.0 us)
Async XLA Ops:
  0.6 9.4 %copy-start.1 = (bf16[2,256,864]{1,2,0:T(8,128)(2,1)S(1)}, bf16[2,256,864]{1,2,0:T(8,128)(2,1)}, u32[]{:S(2)}) copy-start(bf16[2,256,864]{1,2,0:T(8,128)(2,1)} %param.18) | copy-start | bytes 2654212
  0.7 17.8 %collective-permute-start = (s32[512]{0:T(512)}, s32[512]{0:T(512)S(1)}, u32[]{:S(2)}, u32[]{:S(2)}) collective-permute-start(s32[512]{0:T(512)} %param.14), channel_id=1, source_target_pairs={{0,8},{4,12},{8,0},{12,4},{16,24},{20,28},{24,16},{28,20},{1,9},{5... | collective-permute-start | bytes 6152 | tf_op jit(solution)/shard_map/ppermute | solution.py:820
  8.1 5.1 copy-start.2
  8.1 6.1 copy-start.3
  8.1 9.2 %copy-start.4 = (bf16[2,864,256]{2,1,0:T(8,128)(2,1)S(1)}, bf16[2,864,256]{2,1,0:T(8,128)(2,1)}, u32[]{:S(2)}) copy-start(bf16[2,864,256]{2,1,0:T(8,128)(2,1)} %param.24) | copy-start | bytes 2654212
  8.3 10.1 %copy-start.6 = (s32[512]{0:T(512)S(1)}, s32[512]{0:T(512)}, u32[]{:S(2)}) copy-start(s32[512]{0:T(512)} %param.14) | copy-start | bytes 6148
  872.7 8.3 copy-start.5
  872.7 13.4 %copy-start = (f32[128,2048]{1,0:T(8,128)S(1)}, f32[128,2048]{1,0:T(8,128)}, u32[]{:S(2)}) copy-start(f32[128,2048]{1,0:T(8,128)} %get-tuple-element.75) | copy-start | bytes 3145732

commit v2 on v1

--- a/solution.py
+++ b/solution.py
@@ -19,7 +19,13 @@
 MESH = pl.DeviceIdType.MESH
 BF16 = jnp.bfloat16
 F32 = jnp.float32
-LOOK = 3
+LOOK = 2
+SCHED = (
+    ("IIPI", "PI", "", "PI", "PI", ""),
+    ("PI", "PI", "", "PI", "PI", ""),
+    ("PI", "PI", "", "PI", "PI", ""),
+    ("PI", "PI", "", "PI", "PI", ""),
+)
 VMEM_LIMIT = 60 * 1024 * 1024
 
 
@@ -83,7 +89,7 @@
     return pl.ds(pl.multiple_of((half * 4 + tensor) * rows, rows), rows)
 
 
-def gather_acts(me, buf, rows, ssem, rsem, fill=()):
+def gather_acts(me, buf, rows, ssem, rsem, first, second, fill=()):
     fill = list(fill)
 
     def step():
@@ -95,27 +101,32 @@
         return remote(buf.at[r], buf.at[r], ssem.at[k], rsem.at[k], dev)
 
     h, x = me.half, me.x
+    own_z = move(1, h, x, me.znb())
     own_x = move(0, h, x, me.xn())
-    own_z = move(1, h, x, me.znb())
     own_s = move(2, h, x, me.sib())
+    own_z.start()
     own_x.start()
-    own_z.start()
     own_s.start()
     step()
+    own_x.wait_recv()
+    x_s = move(5, h, 1 - x, me.sib())
+    x_s.start()
     own_z.wait_recv()
     z_x = move(3, 1 - h, x, me.xn())
     z_s = move(4, 1 - h, x, me.sib())
     z_x.start()
     z_s.start()
-    own_x.wait_recv()
-    x_s = move(5, h, 1 - x, me.sib())
-    x_s.start()
     step()
+    own_s.wait_recv()
+    x_s.wait_recv()
+    first(h)
     z_x.wait_recv()
     g_s = move(6, 1 - h, 1 - x, me.sib())
     g_s.start()
-    for m in (own_s, z_s, x_s, g_s):
-        m.wait_recv()
+    step()
+    z_s.wait_recv()
+    g_s.wait_recv()
+    second(1 - h)
     for m in (own_x, own_z, own_s, z_x, z_s, x_s, g_s):
         m.wait_send()
     while fill:
@@ -136,6 +147,7 @@
         m = remote(part.at[block(hh, xx * 2 + 1 - me.c, rows)], sib_buf.at[j], ssem.at[j], rsem.at[j], me.sib())
         m.start()
         sibs.append(m)
+    step()
     chunk = 64
 
     def mine(j, i):
@@ -205,7 +217,7 @@
 
 def forward_kernel(
     dims,
-    tokens, mask, cosine, sine, attn_gain, ffn_gain, wl,
+    tokens, mask, cosine, sine, attn_gain, ffn_gain, w_q, w_k, w_v, w_s, w_o, w_g, w_u, w_d,
     output, x_mid, mids, wf, s_n, s_nf, s_q, s_k, s_v, s_s, s_m, s_gt, s_g, s_u, s_h, s_p,
     W, N0, N1, part, sib_buf, x_buf, z_buf, q, k, v, s, m, gt, g, u, h, p,
     zs, zr, ys, yr, lo, ld, ags, agr, rss, rsr, sv,
@@ -213,15 +225,20 @@
     layers, rows, lanes, units, scale = dims
     me = Place()
     names = list(units)
+    shards = dict(q=w_q, k=w_k, v=w_v, s=w_s, o=w_o, g=w_g, u=w_u, d=w_d)
     groups = [(l, units[n]) for l in range(layers) for n in names]
     spot = {(l, n): l * len(names) + i for l in range(layers) for i, n in enumerate(names)}
     my_lane = pl.multiple_of(me.dp * lanes, lanes)
+
+    def shard(i, half):
+        n = groups[i][1][1]
+        return shards[names[i % len(names)]].at[groups[i][0], pl.ds(pl.multiple_of(half * n, 16), n)]
 
     def z_copy(i, d):
         l, (r0, n) = groups[i]
         tz = me.zplus(d)
         return remote(
-            wl.at[l, lax.rem(tz, 2), pl.ds(r0, n)], wf.at[l, pl.ds(r0, n), pl.ds(my_lane, lanes)],
+            shard(i, lax.rem(tz, 2)), wf.at[l, pl.ds(r0, n), pl.ds(my_lane, lanes)],
             zs.at[i, d - 1], zr.at[i, d - 1], me.at(z=tz),
         )
 
@@ -229,13 +246,13 @@
         l, (r0, n) = groups[i]
         lane = pl.ds(pl.multiple_of((me.zplus(-d) * 2 + me.y) * lanes, lanes), lanes)
         dst = wf.at[l, pl.ds(r0, n), lane]
-        src = wl.at[l, me.half, pl.ds(r0, n)] if d == 0 else dst
+        src = shard(i, me.half) if d == 0 else dst
         return remote(src, dst, ys.at[i, d], yr.at[i, d], me.yn())
 
     def local_copy(i):
         l, (r0, n) = groups[i]
         return pltpu.make_async_copy(
-            wl.at[l, me.half, pl.ds(r0, n)], wf.at[l, pl.ds(r0, n), pl.ds(my_lane, lanes)], lo.at[i]
+            shard(i, me.half), wf.at[l, pl.ds(r0, n), pl.ds(my_lane, lanes)], lo.at[i]
         )
 
     def issue(i):
@@ -245,22 +262,49 @@
             y_copy(i, 0).start()
             local_copy(i).start()
 
-    done = [0]
-
-    def advance():
-        i = done[0]
+    issued, pumped = [0], [0]
+
+    def send_next():
+        if issued[0] < len(groups):
+            issue(issued[0])
+            issued[0] += 1
+
+    def pass_on():
+        i = pumped[0]
         if i >= len(groups):
             return
-        done[0] += 1
+        while issued[0] <= i:
+            send_next()
+        pumped[0] += 1
         for d in (1, 3, 2):
             z_copy(i, d).wait_recv()
             y_copy(i, d).start()
-        issue(i + LOOK)
+
+    plan = SCHED
+
+    def act(pair, point):
+        def go():
+            for ch in plan[pair][point]:
+                if ch == "I":
+                    send_next()
+                if ch == "P":
+                    pass_on()
+        return go
+
+    def gfill(pair):
+        return [act(pair, 0), act(pair, 1), act(pair, 5)]
+
+    def sfill(pair):
+        return [act(pair, 2), act(pair, 3), act(pair, 4)]
 
     def take(l, *wanted):
         idx = [spot[l, n] for n in wanted]
-        while done[0] <= min(idx[-1] + 1, len(groups) - 1):
-            advance()
+        while pumped[0] <= idx[-1]:
+            pass_on()
+            while issued[0] - pumped[0] < LOOK:
+                if issued[0] >= len(groups):
+                    break
+                send_next()
         copies = []
         for i in idx:
             for d in range(4):
@@ -301,9 +345,6 @@
         return pl.ds(pl.multiple_of(own + r0, n), n)
 
     me.greet()
-    for i in range(LOOK):
-        issue(i)
-
     small = 32
 
     def first_norm(i):
@@ -313,62 +354,61 @@
 
     loop(rows // small, first_norm)
 
+    def out_rows(i, src, name):
+        def go(j):
+            r = pl.ds(pl.multiple_of(i * LEN + j * 256, 256), 256)
+            part[r, :] = dot(src[r, :], weight(name)).astype(BF16)
+
+        loop(LEN // 256, go)
+
+    def attn_seq(i, l, fetch):
+        def get(name):
+            if fetch:
+                take(l, name)
+
+        r = seq_rows(i)
+        for name, dst in (("q", q), ("k", k)):
+            get(name)
+            t = dot(N0[r, :], weight(name), NT)
+            half = t.shape[1] // 2
+            t1, t2 = t[:, :half], t[:, half:]
+            c, sn = cosine[...], sine[...]
+            dst[r, :half] = (t1 * c - t2 * sn).astype(BF16)
+            dst[r, half:] = (t2 * c + t1 * sn).astype(BF16)
+        get("v")
+        v[r, :] = dot(N0[r, :], weight("v"), NT).astype(BF16)
+        raw = dot(q[r, :], k[r, :], NT) * scale
+        probs = (raw * mask[i]).astype(BF16)
+        p[i] = probs
+        m[r, :] = dot(probs, v[r, :])
+        get("s")
+        t = dot(N0[r, :], weight("s"), NT)
+        s[r, :] = t
+        mix = m[r, :]
+        gt[r, :] = (jax.nn.silu(t) * (mix * rms(mix, HEAD_FLOOR))).astype(BF16)
+        get("o")
+        out_rows(i, gt, "o")
+
+    def ffn_seq(i, l, fetch):
+        r = seq_rows(i)
+        if fetch:
+            take(l, "g")
+        g[r, :] = dot(N1[r, :], weight("g"), NT)
+        if fetch:
+            take(l, "u")
+        t = dot(N1[r, :], weight("u"), NT)
+        u[r, :] = t
+        h[r, :] = (jax.nn.gelu(g[r, :], approximate=True) * t).astype(BF16)
+        if fetch:
+            take(l, "d")
+        out_rows(i, h, "d")
+
+    both = lambda body, l: (functools.partial(body, l=l, fetch=True), functools.partial(body, l=l, fetch=False))
+
     for l in range(layers):
-        gather_acts(me, N0, rows, ags.at[2 * l], agr.at[2 * l], (advance,))
-        save(N0, s_n.at[l])
-        for name, dst in (("q", q), ("k", k)):
-            take(l, name)
-
-            def project(i, name=name, dst=dst):
-                r = seq_rows(i)
-                t = dot(N0[r, :], weight(name), NT)
-                half = t.shape[1] // 2
-                t1, t2 = t[:, :half], t[:, half:]
-                c, sn = cosine[...], sine[...]
-                dst[r, :half] = (t1 * c - t2 * sn).astype(BF16)
-                dst[r, half:] = (t2 * c + t1 * sn).astype(BF16)
-
-            loop(seqs, project)
-        save(q, s_q.at[l])
-        save(k, s_k.at[l])
-        take(l, "v")
-
-        def values(i):
-            r = seq_rows(i)
-            v[r, :] = dot(N0[r, :], weight("v"), NT).astype(BF16)
-
-        loop(seqs, values)
-        save(v, s_v.at[l])
-
-        def retain(i):
-            r = seq_rows(i)
-            raw = dot(q[r, :], k[r, :], NT) * scale
-            probs = (raw * mask[i]).astype(BF16)
-            p[i] = probs
-            m[r, :] = dot(probs, v[r, :])
-
-        loop(seqs, retain)
-        save(p, s_p.at[l])
-        save(m, s_m.at[l])
-        take(l, "s")
-
-        def gate(i):
-            r = seq_rows(i)
-            t = dot(N0[r, :], weight("s"), NT)
-            s[r, :] = t
-            mix = m[r, :]
-            gt[r, :] = (jax.nn.silu(t) * (mix * rms(mix, HEAD_FLOOR))).astype(BF16)
-
-        loop(seqs, gate)
-        save(s, s_s.at[l])
-        save(gt, s_gt.at[l])
-        take(l, "o")
-
-        def project_out(i, src=gt, name="o"):
-            r = pl.ds(pl.multiple_of(i * 256, 256), 256)
-            part[r, :] = dot(src[r, :], weight(name)).astype(BF16)
-
-        loop(seqs * LEN // 256, project_out)
+        gather_acts(me, N0, rows, ags.at[2 * l], agr.at[2 * l], *both(attn_seq, l), gfill(2 * l))
+        for src, dst in ((N0, s_n), (q, s_q), (k, s_k), (v, s_v), (p, s_p), (m, s_m), (s, s_s), (gt, s_gt)):
+            save(src, dst.at[l])
 
         def to_mid(r0, n, total, l=l):
             r = pl.ds(pl.multiple_of(r0, n), n)
@@ -376,30 +416,10 @@
             mids[l, r, :] = x
             N1[own_rows(r0, n), :] = (x * rms(x, EPS) * ffn_gain[l : l + 1, :]).astype(BF16)
 
-        sum_acts(me, part, rows, sib_buf, x_buf, z_buf, rss.at[2 * l], rsr.at[2 * l], to_mid, (advance,))
-        gather_acts(me, N1, rows, ags.at[2 * l + 1], agr.at[2 * l + 1], (advance,))
-        save(N1, s_nf.at[l])
-        take(l, "g")
-
-        def gates(i):
-            r = seq_rows(i)
-            g[r, :] = dot(N1[r, :], weight("g"), NT)
-
-        loop(seqs, gates)
-        take(l, "u")
-
-        def ups(i):
-            r = seq_rows(i)
-            t = dot(N1[r, :], weight("u"), NT)
-            u[r, :] = t
-            h[r, :] = (jax.nn.gelu(g[r, :], approximate=True) * t).astype(BF16)
-
-        loop(seqs, ups)
-        save(g, s_g.at[l])
-        save(u, s_u.at[l])
-        save(h, s_h.at[l])
-        take(l, "d")
-        loop(seqs * LEN // 256, functools.partial(project_out, src=h, name="d"))
+        sum_acts(me, part, rows, sib_buf, x_buf, z_buf, rss.at[2 * l], rsr.at[2 * l], to_mid, sfill(2 * l))
+        gather_acts(me, N1, rows, ags.at[2 * l + 1], agr.at[2 * l + 1], *both(ffn_seq, l), gfill(2 * l + 1))
+        for src, dst in ((N1, s_nf), (g, s_g), (u, s_u), (h, s_h)):
+            save(src, dst.at[l])
 
         def to_next(r0, n, total, l=l):
             r = pl.ds(pl.multiple_of(r0, n), n)
@@ -411,7 +431,7 @@
                 output[r, :] = x.astype(BF16)
 
         settle()
-        sum_acts(me, part, rows, sib_buf, x_buf, z_buf, rss.at[2 * l + 1], rsr.at[2 * l + 1], to_next, (advance,))
+        sum_acts(me, part, rows, sib_buf, x_buf, z_buf, rss.at[2 * l + 1], rsr.at[2 * l + 1], to_next, sfill(2 * l + 1))
     settle()
     for i in range(len(groups)):
         for d in (1, 2, 3):
@@ -420,10 +440,9 @@
             y_copy(i, d).wait_send()
 
 
-def run_forward(dims, tokens, mask, cosine, sine, attn_gain, ffn_gain, wl):
+def run_forward(dims, total, tokens, mask, cosine, sine, attn_gain, ffn_gain, weights):
     layers, rows, lanes, units, scale = dims
     depth = tokens.shape[1]
-    total = wl.shape[2]
     group = 8 * rows
     seqs = group // LEN
     qk, val, ffn = units["q"][1], units["v"][1], units["g"][1]
@@ -442,7 +461,7 @@
     return pl.pallas_call(
         functools.partial(forward_kernel, dims),
         out_shape=[jax.ShapeDtypeStruct(s, d) for s, d in outs],
-        in_specs=[vm] * 6 + [hb],
+        in_specs=[vm] * 6 + [hb] * 8,
         out_specs=[vm] * 3 + [hb] * 13,
         scratch_shapes=[
             pltpu.VMEM((total, depth), BF16),
@@ -458,10 +477,16 @@
             dma((12 * layers,)),
         ],
         compiler_params=pltpu.CompilerParams(collective_id=0, has_side_effects=True, vmem_limit_bytes=VMEM_LIMIT),
-    )(tokens, mask, cosine, sine, attn_gain, ffn_gain, wl)
+    )(tokens, mask, cosine, sine, attn_gain, ffn_gain, *weights)
 
 
 SLOTS = 4
+BSCHED = (
+    ("", "", "", "", "M", "MM", ""),
+    ("C", "C", "", "", "CMM", "CMCMM", ""),
+    ("C", "C", "C", "", "M", "MM", ""),
+    ("C", "C", "", "", "CMM", "CMCMM", ""),
+)
 
 
 def backward_kernel(
@@ -469,7 +494,7 @@
     cot, tokens, x_mid, mids, mask, cosine, sine, attn_gain, ffn_gain,
     wf, s_n, s_nf, s_q, s_k, s_v, s_s, s_m, s_gt, s_g, s_u, s_h, s_p,
     input_grad, gains, rz,
-    gr, nb, ga0, ga1, part, sib_buf, x_buf, z_buf, W, a1, a2, a3, q, k, v, p, t1, t2, tq, tk, G, ry, acc, acc_in,
+    gr, xb, nb, ga0, ga1, part, sib_buf, x_buf, z_buf, W, a1, a2, a3, q, k, v, p, t1, t2, tq, tk, G, ry, acc, acc_in,
     ys, yr, zs, zr, os, ags, agr, rss, rsr, ld, gns, gnr, credit,
 ):
     layers, rows, lanes, units, scale = dims
@@ -588,6 +613,9 @@
         load(("v", l), s_v.at[l], v)
         load(("p", l), s_p.at[l], p)
 
+    def load_mid(l):
+        load(("mid", l), mids.at[l], xb)
+
     def load_h(l):
         load(("h", l), s_h.at[l], a3)
 
@@ -613,6 +641,7 @@
 
     me.greet()
     load_ffn(order[0])
+    load_mid(order[0])
     load_h(order[0])
     load_nf(order[0])
     acc[0] = jnp.zeros(acc.shape[1:], F32)
@@ -623,14 +652,65 @@
         ga0[own_rows(i * small, small), :] = cot[r, :]
 
     loop(rows // small, begin)
-    later = []
-    for at, l in enumerate(order):
-        last = at == layers - 1
-        gather_acts(me, ga0, rows, ags.at[2 * at], agr.at[2 * at], later)
-        ready(("wf", l), ("g", l), ("u", l))
-
-        def ffn_back(i):
-            r = seq_rows(i)
+
+    jobs_of = {
+        "d": (a3, ga0, ("h",), lambda l: load_gt(l)),
+        "g": (t1, nb, ("nf",), None),
+        "u": (t2, nb, (), lambda l: load_n(l)),
+        "o": (a3, ga1, ("gt",), None),
+        "q": (tq, nb, ("n",), None),
+        "k": (tk, nb, (), None),
+        "v": (t1, nb, (), None),
+        "s": (t2, nb, (), lambda l: (load_nf(l - 1), load_h(l - 1)) if l else None),
+    }
+    open_to, made, added = [0], [0], [0]
+
+    def add_next():
+        if added[0] < made[0]:
+            combine(*jobs[added[0]])
+            added[0] += 1
+
+    def make_next():
+        if made[0] < open_to[0]:
+            i = made[0]
+            while added[0] <= i - SLOTS:
+                add_next()
+            l, name = jobs[i]
+            left, right, needs, then = jobs_of[name]
+            ready(*((key, l) for key in needs))
+            make(l, name, left, right)
+            made[0] += 1
+            if then:
+                then(l)
+
+    def make_all():
+        while made[0] < open_to[0]:
+            make_next()
+
+    plan = BSCHED
+
+    def act(pair, point):
+        def go():
+            for ch in plan[pair][point]:
+                if ch == "M":
+                    make_next()
+                if ch == "C":
+                    add_next()
+
+        return go
+
+    def gfill(pair):
+        return [act(pair, i) for i in (0, 1, 2)]
+
+    def sfill(pair):
+        return [act(pair, i) for i in (3, 4, 5, 6)]
+
+    def tile_rows(i, j):
+        return pl.ds(pl.multiple_of(i * LEN + j * 256, 256), 256)
+
+    def ffn_seq(i):
+        def go(j):
+            r = tile_rows(i, j)
             gh = dot(ga0[r, :], weight("d", ffn_row), NT)
             g, u = a1[r, :], a2[r, :]
             th = jnp.tanh(0.7978845608028654 * (g + 0.044715 * g * g * g))
@@ -638,42 +718,13 @@
             slope = 0.5 * (1.0 + th) + 0.5 * g * (1.0 - th * th) * (0.7978845608028654 * (1.0 + 0.134145 * g * g))
             t1[r, :] = (gh * u * slope).astype(BF16)
             t2[r, :] = (gh * val).astype(BF16)
-
-        loop(seqs, ffn_back)
-
-        def ffn_sum(i):
-            r = pl.ds(pl.multiple_of(i * 256, 256), 256)
             part[r, :] = (dot(t1[r, :], weight("g", ffn_row)) + dot(t2[r, :], weight("u", ffn_row))).astype(BF16)
 
-        loop(seqs * LEN // 256, ffn_sum)
-        load_attn(l)
-        ready(("h", l), ("nf", l))
-
-        def fill_d(l=l):
-            make(l, "d", a3, ga0)
-            load_gt(l)
-
-        def fill_gu(l=l):
-            make(l, "g", t1, nb)
-            make(l, "u", t2, nb)
-            load_n(l)
-
-        def to_mid(r0, n, tot, l=l):
-            r = pl.ds(pl.multiple_of(r0, n), n)
-            new = gr[r, :] + norm_back(mids[l, r, :], ffn_gain[l : l + 1, :], tot, layers + l)
-            gr[r, :] = new
-            ga1[own_rows(r0, n), :] = new.astype(BF16)
-
-        sum_acts(me, part, rows, sib_buf, x_buf, z_buf, rss.at[2 * at], rsr.at[2 * at], to_mid, (fill_d, fill_gu))
-        mids_of = functools.partial
-        gather_acts(
-            me, ga1, rows, ags.at[2 * at + 1], agr.at[2 * at + 1],
-            (mids_of(combine, l, "d"), mids_of(combine, l, "g")),
-        )
-        ready(("wa", l), ("s", l), ("m", l), ("q", l), ("k", l), ("v", l), ("p", l))
-
-        def attn_back(i):
-            r = seq_rows(i)
+        loop(LEN // 256, go)
+
+    def attn_head(i):
+        def go(j):
+            r = tile_rows(i, j)
             gg = dot(ga1[r, :], weight("o", 0), NT)
             s, mix = a1[r, :], a2[r, :]
             sig = 1.0 / (1.0 + jnp.exp(-s))
@@ -681,47 +732,67 @@
             t2[r, :] = (gg * (mix * rr) * (sig * (1.0 + s * (1.0 - sig)))).astype(BF16)
             gz = gg * (s * sig)
             inner = jnp.sum(gz * mix, -1, keepdims=True) / mix.shape[1]
-            gm = (rr * gz - (rr * rr * rr) * mix * inner).astype(BF16)
-            raw = (dot(gm, v[r, :], NT) * mask[i]).astype(BF16)
-            t1[r, :] = dot(p[i], gm, TN).astype(BF16)
-            c, sn = cosine[...], sine[...]
-            for dst, grad in ((tq, dot(raw, k[r, :]) * scale), (tk, dot(raw, q[r, :], TN) * scale)):
-                half = grad.shape[1] // 2
-                g1, g2 = grad[:, :half], grad[:, half:]
-                dst[r, :half] = (g1 * c + g2 * sn).astype(BF16)
-                dst[r, half:] = (g2 * c - g1 * sn).astype(BF16)
-
-        loop(seqs, attn_back)
-
-        def attn_sum(i):
-            r = pl.ds(pl.multiple_of(i * 256, 256), 256)
+            t1[r, :] = (rr * gz - (rr * rr * rr) * mix * inner).astype(BF16)
+
+        loop(LEN // 256, go)
+
+    def attn_tail(i):
+        r = seq_rows(i)
+        gm = t1[r, :]
+        raw = (dot(gm, v[r, :], NT) * mask[i]).astype(BF16)
+        t1[r, :] = dot(p[i], gm, TN).astype(BF16)
+        c, sn = cosine[...], sine[...]
+        for dst, grad in ((tq, dot(raw, k[r, :]) * scale), (tk, dot(raw, q[r, :], TN) * scale)):
+            half = grad.shape[1] // 2
+            g1, g2 = grad[:, :half], grad[:, half:]
+            dst[r, :half] = (g1 * c + g2 * sn).astype(BF16)
+            dst[r, half:] = (g2 * c - g1 * sn).astype(BF16)
+
+        def go(j):
+            r = pl.ds(pl.multiple_of(i * LEN + j * 256, 256), 256)
             tot = dot(tq[r, :], weight("q", 0)) + dot(tk[r, :], weight("k", 0))
             tot = tot + dot(t1[r, :], weight("v", 0)) + dot(t2[r, :], weight("s", 0))
             part[r, :] = tot.astype(BF16)
 
-        loop(seqs * LEN // 256, attn_sum)
+        loop(LEN // 256, go)
+
+    def attn_seq(i):
+        attn_head(i)
+        attn_tail(i)
+
+    def after(keys, body):
+        def go(i):
+            make_all()
+            ready(*keys)
+            body(i)
+
+        return go
+
+    for at, l in enumerate(order):
+        last = at == layers - 1
+        first = after([("wf", l), ("g", l), ("u", l), ("mid", l)], ffn_seq)
+        gather_acts(me, ga0, rows, ags.at[2 * at], agr.at[2 * at], first, ffn_seq, gfill(2 * at))
+        load_attn(l)
+        open_to[0] = 8 * at + 3
+
+        def to_mid(r0, n, tot, l=l):
+            r = pl.ds(pl.multiple_of(r0, n), n)
+            new = gr[r, :] + norm_back(xb[r, :], ffn_gain[l : l + 1, :], tot, layers + l)
+            gr[r, :] = new
+            ga1[own_rows(r0, n), :] = new.astype(BF16)
+
+        sum_acts(me, part, rows, sib_buf, x_buf, z_buf, rss.at[2 * at], rsr.at[2 * at], to_mid, sfill(2 * at))
+        if l:
+            load(("x", l), x_mid.at[l - 1], xb)
+        first = after([(key, l) for key in ("wa", "s", "m", "q", "k", "v", "p") + (("x",) if l else ())], attn_seq)
+        gather_acts(me, ga1, rows, ags.at[2 * at + 1], agr.at[2 * at + 1], first, attn_seq, gfill(2 * at + 1))
         if not last:
             load_ffn(order[at + 1])
-        ready(("gt", l), ("n", l))
-
-        def fill_o(l=l):
-            combine(l, "u")
-            make(l, "o", a3, ga1)
-            make(l, "q", tq, nb)
-
-        def fill_kv(l=l, last=last):
-            combine(l, "o")
-            make(l, "k", tk, nb)
-            combine(l, "q")
-            make(l, "v", t1, nb)
-            make(l, "s", t2, nb)
-            if not last:
-                load_nf(l - 1)
-                load_h(l - 1)
+        open_to[0] = 8 * at + 8
 
         def to_prev(r0, n, tot, l=l, last=last):
             r = pl.ds(pl.multiple_of(r0, n), n)
-            x = tokens[r, :].astype(F32) if l == 0 else x_mid[l - 1, r, :]
+            x = tokens[r, :].astype(F32) if l == 0 else xb[r, :]
             new = gr[r, :] + norm_back(x, attn_gain[l : l + 1, :], tot, l)
             if last:
                 input_grad[r, :] = new
@@ -729,11 +800,15 @@
                 gr[r, :] = new
                 ga0[own_rows(r0, n), :] = new.astype(BF16)
 
-        sum_acts(me, part, rows, sib_buf, x_buf, z_buf, rss.at[2 * at + 1], rsr.at[2 * at + 1], to_prev, (fill_o, fill_kv))
-        later = [mids_of(combine, l, "k"), mids_of(combine, l, "v"), mids_of(combine, l, "s")]
-
-    for go in later:
-        go()
+        sum_acts(
+            me, part, rows, sib_buf, x_buf, z_buf, rss.at[2 * at + 1], rsr.at[2 * at + 1], to_prev, sfill(2 * at + 1)
+        )
+        if not last:
+            load_mid(order[at + 1])
+
+    make_all()
+    while added[0] < made[0]:
+        add_next()
     partners = [me.sib(), me.xn(), me.yn(), me.znb(), me.at(z=me.zplus(2))]
     for j, dev in enumerate(partners):
         m = remote(acc.at[j], acc_in.at[j], gns.at[j], gnr.at[j], dev)
@@ -766,10 +841,10 @@
     return pl.pallas_call(
         functools.partial(backward_kernel, dims),
         out_shape=[jax.ShapeDtypeStruct(s, d) for s, d in outs],
-        in_specs=[vm] * 9 + [hb] * 13,
+        in_specs=[vm, vm, hb, hb] + [vm] * 5 + [hb] * 13,
         out_specs=[vm] * 2 + [hb],
         scratch_shapes=[
-            pltpu.VMEM((rows, depth), F32), big, big, big, big,
+            pltpu.VMEM((rows, depth), F32), pltpu.VMEM((rows, depth), F32), big, big, big, big,
             pltpu.VMEM((4, rows, depth), BF16), pltpu.VMEM((2, rows, depth), BF16), pltpu.VMEM((rows, depth), BF16),
             pltpu.VMEM((max(attn_rows, total - attn_rows), depth), BF16),
             pltpu.VMEM((group, val), F32), pltpu.VMEM((group, val), F32), pltpu.VMEM((group, val), BF16),
@@ -786,6 +861,42 @@
         compiler_params=pltpu.CompilerParams(collective_id=1, has_side_effects=True, vmem_limit_bytes=VMEM_LIMIT),
     )(cot, tokens, x_mid, mids, mask, cosine, sine, attn_gain, ffn_gain, *kept)
 
+
+NAMES = ("q", "k", "v", "s", "o", "g", "u", "d")
+TILE = 128
+
+
+def unstack_kernel(units, parts, *outs):
+    for name, out in zip(NAMES, outs):
+        r0, n = units[name]
+        both = [parts[0, h, 0, r0 : r0 + n].astype(F32) + parts[0, h, 1, r0 : r0 + n].astype(F32) for h in range(2)]
+        if name in ("q", "k"):
+            out[0] = jnp.concatenate(both, 0).T
+        else:
+            for h in range(2):
+                out[0, h * n : (h + 1) * n] = both[h]
+
+
+def unstack_grads(units, parts):
+    layers, _, _, total, lanes = parts.shape
+    shapes, specs = [], []
+    for name in NAMES:
+        n = 2 * units[name][1]
+        if name in ("q", "k"):
+            shapes.append((layers, lanes, n))
+            specs.append(pl.BlockSpec((1, TILE, n), lambda l, j: (l, j, 0)))
+        else:
+            shapes.append((layers, n, lanes))
+            specs.append(pl.BlockSpec((1, n, TILE), lambda l, j: (l, 0, j)))
+    return pl.pallas_call(
+        functools.partial(unstack_kernel, units),
+        grid=(layers, lanes // TILE),
+        in_specs=[pl.BlockSpec((1, 2, 2, total, TILE), lambda l, j: (l, 0, 0, 0, j))],
+        out_specs=specs,
+        out_shape=[jax.ShapeDtypeStruct(s, F32) for s in shapes],
+        compiler_params=pltpu.CompilerParams(vmem_limit_bytes=VMEM_LIMIT),
+    )(parts)
+
 def rotation(length, width):
     half = width // 2
     place = jnp.arange(length, dtype=F32)
@@ -801,17 +912,6 @@
     rate = jnp.log1p(-(2.0 ** (-5.0 - head)))
     decay = jnp.exp(jnp.maximum(dist, 0).astype(F32) * rate)
     return jnp.where(same, decay[None], 0.0)
-
-
-def stack_weights(w_query, w_key, w_value, w_swish, w_output, w_gelu, w_up, w_down):
-    def cut(w):
-        return w.reshape(w.shape[0], 2, w.shape[1] // 2, w.shape[2])
-
-    def turn(w):
-        return cut(jnp.swapaxes(w, 1, 2))
-
-    parts = [turn(w_query), turn(w_key), turn(w_value), turn(w_swish), cut(w_output), turn(w_gelu), turn(w_up), cut(w_down)]
-    return jnp.concatenate(parts, axis=2)
 
 
 def setup(segments, w_query, w_value, w_gelu):
@@ -822,7 +922,7 @@
     mask = decay_mask(pair, (tensor * 2 + half).astype(F32), LEN)
     cosine, sine = rotation(LEN, HEAD_QK)
     units, total = unit_rows(w_query.shape[2] // 2, w_value.shape[2] // 2, w_gelu.shape[2] // 2)
-    return mask, cosine, sine, units
+    return mask, cosine, sine, units, total
 
 
 CONTRACT_ROWS = (((0,), (0,)), ((), ()))
@@ -1122,26 +1222,21 @@
     tokens, segments, attn_gain, w_query, w_key, w_value, w_swish, w_output, ffn_gain, w_gelu, w_up, w_down, cotangent
 ):
     layers = w_query.shape[0]
-    mask, cosine, sine, units = setup(segments, w_query, w_value, w_gelu)
-    wl = stack_weights(w_query, w_key, w_value, w_swish, w_output, w_gelu, w_up, w_down)
+    mask, cosine, sine, units, total = setup(segments, w_query, w_value, w_gelu)
+    turn = lambda w: jnp.swapaxes(w, 1, 2)
+    weights = (
+        turn(w_query), turn(w_key), turn(w_value), turn(w_swish), w_output, turn(w_gelu), turn(w_up), w_down,
+    )
     dims = (layers, tokens.shape[0], w_query.shape[1], units, HEAD_QK ** (-0.5))
-    output, x_mid, mids, *kept = run_forward(dims, tokens, mask, cosine, sine, attn_gain, ffn_gain, wl)
-    input_grad, gains, rz = run_backward(
+    output, x_mid, mids, *kept = run_forward(
+        dims, total, tokens, mask, cosine, sine, attn_gain, ffn_gain, weights
+    )
+    input_grad, gains, parts = run_backward(
         dims, cotangent, tokens, x_mid, mids, mask, cosine, sine, attn_gain, ffn_gain, kept
     )
-    sums = rz[:, :, 0].astype(F32) + rz[:, :, 1].astype(F32)
-
-    def piece(name):
-        r0, n = units[name]
-        part = sums[:, :, r0 : r0 + n]
-        return part.reshape(layers, 2 * n, part.shape[3])
-
-    def turned(name):
-        return jnp.swapaxes(piece(name), 1, 2)
-
+    q, k, v, s, o, g, u, d = unstack_grads(units, parts)
     return (
-        output, input_grad, gains[:layers], turned("q"), turned("k"), turned("v"), turned("s"), piece("o"),
-        gains[layers : 2 * layers], turned("g"), turned("u"), piece("d"),
+        output, input_grad, gains[:layers], q, k, turn(v), turn(s), o, gains[layers : 2 * layers], turn(g), turn(u), d,
     )
 
 

time: 897 us -> 784 us (0.87)
  Pallas kernels: 840 us -> 758 us
  local copies, waits for them, and re-layouts: 28.7 us -> 5.32 us
  other arithmetic: 14.3 us -> 3.81 us
    pallas_call x1, Pallas kernels: 439 us -> 383 us  [run_forward(): pl.pallas_call(functools.partial(forward_kernel, dims), out_shape=[jax.Sh...]
    pallas_call x1, Pallas kernels: 401 us -> 365 us  [run_backward(): pl.pallas_call(functools.partial(backward_kernel, dims), out_shape=[jax.S...]
    add x1 -> x0, other arithmetic: 10.5 us -> none  [grouped(): sums = rz[:, :, 0].astype(F32) + rz[:, :, 1].astype(F32)]
    slice x2 -> x0, local copies, waits for them, and re-layouts: 10.1 us -> none  [piece(): part = sums[:, :, r0:r0 + n]]
    pallas_call x0 -> x1, Pallas kernels: none -> 9.41 us  [unstack_grads(): pl.pallas_call(functools.partial(unstack_kernel, units), grid=(layers, la...]
  transfers between devices with their start and end apart: 1 -> 1, of which waited for: 0 -> 0; matrix products, arithmetic and copies ran while one was open for 2% -> 1% of each run, Pallas kernels for 0% -> 0%
where the time goes in v2:
time: 784 us; the launch traced here: 772 us
  Pallas kernels  758 us (97%)
    pallas_call x1, Pallas kernels, run_forward(): pl.pallas_call(functools.partial(forward_kernel, dims), out_shape=[jax.Sh...  383 us
    pallas_call x1, Pallas kernels, run_backward(): pl.pallas_call(functools.partial(backward_kernel, dims), out_shape=[jax.S...  365 us
  transfers between devices with their start and end apart: 1, of which 0 were waited for; matrix products, arithmetic and copies ran while one was open for 1% of the time, Pallas kernels for 0%

profile of v2, /device:TPU:0, one launch (start us, length us, event | category | flops | bytes accessed | tf_op | source)
XLA Modules:
  0.0 771.6 jit_solution(6576137135248243802)
XLA Ops:
  0.6 0.0 copy-start.4
  0.7 0.0 copy-start.1
  0.7 0.0 copy-start.2
  0.7 3.1 collective-permute-start
  3.9 1.7 fusion.1
  5.6 0.2 multiply_exponential_fusion
  5.8 0.1 fusion
  5.9 0.0 copy-done.1
  5.9 1.0 copy.25
  6.9 0.0 copy-done.2
  6.9 1.0 copy.26
  7.9 0.0 collective-permute-done
  7.9 0.0 copy-done.4
  7.9 1.8 and_select_fusion.mask
  9.7 383.5 %shard_map.220 = (bf16[128,2048]{1,0:T(8,128)(2,1)}, f32[1,128,2048]{2,1,0:T(8,128)}, f32[2,128,2048]{2,1,0:T(8,128)}, bf16[2,3104,2048]{2,1,0:T(8,128)(2,1)}, b...) custom-call(bf16[128,2048]{1,0:T(8,128)(2,1)} %tokens.3, ...), custom_call_target="tpu_custom_call" | custom-call | tf_op jit(solution)/shard_map/pallas_call | solution.py:461
  393.2 365.2 %shard_map.221 = (f32[128,2048]{1,0:T(8,128)}, f32[8,2048]{1,0:T(8,128)}, bf16[2,2,2,3104,256]{4,3,2,1,0:T(8,128)(2,1)}) custom-call(bf16[128,2048]{1,0:T(8,128)(2,1)} %cot.1, bf16[128,2048]{1,0:T(8,128)(2,1)} %tokens.3, f32[1,128,2048]{2,1,0:T(8,128)} %get-tuple-element.40.x_mid, f32[2,128,2048]{2,1,0:T(8,128)} %get-tuple-element.41.mids, ...), custom_call_target="tpu_custom_call" | custom-call | tf_op jit(solution)/shard_map/pallas_call | solution.py:841
  758.4 1.5 fusion.3
  760.0 0.0 copy-start.3
  760.0 0.0 copy-start
  760.0 9.4 %shard_map.222 = (f32[2,256,512]{2,1,0:T(8,128)}, f32[2,256,512]{2,1,0:T(8,128)}, f32[2,864,256]{2,1,0:T(8,128)}, f32[2,864,256]{2,1,0:T(8,128)}, f32[2,864,256]...) custom-call(bf16[2,2,2,3104,256]{4,3,2,1,0:T(8,128)(2,1)} %get-tuple-element.57.parts), custom_call_target="tpu_custom_call" | custom-call | tf_op jit(solution)/shard_map/pallas_call | solution.py:891
  769.4 0.0 copy-done.3
  769.4 0.8 copy.29
  770.2 0.0 copy-done
  770.2 1.0 copy.30
  (2 shorter events, 0.0 us)
Async XLA Ops:
  0.6 7.3 copy-start.4
  0.7 5.2 copy-start.1
  0.7 6.2 copy-start.2
  0.7 7.2 collective-permute-start
  760.0 9.4 %copy-start.3 = (bf16[128,2048]{1,0:T(8,128)(2,1)S(1)}, bf16[128,2048]{1,0:T(8,128)(2,1)}, u32[]{:S(2)}) copy-start(bf16[128,2048]{1,0:T(8,128)(2,1)} %get-tuple-element.82) | copy-start | bytes 1572868
  760.0 10.2 %copy-start = (f32[128,2048]{1,0:T(8,128)S(1)}, f32[128,2048]{1,0:T(8,128)}, u32[]{:S(2)}) copy-start(f32[128,2048]{1,0:T(8,128)} %get-tuple-element.83) | copy-start | bytes 3145732

commit v3 on v2

--- a/solution.py
+++ b/solution.py
@@ -21,11 +21,14 @@
 F32 = jnp.float32
 LOOK = 2
 SCHED = (
-    ("IIPI", "PI", "", "PI", "PI", ""),
+    ("III", "P", "", "PI", "PI", "PI"),
     ("PI", "PI", "", "PI", "PI", ""),
     ("PI", "PI", "", "PI", "PI", ""),
     ("PI", "PI", "", "PI", "PI", ""),
+    ("PI", "PI", "", "", ""),
 )
+COT_AFTER = "v"
+CHUNKS = 2
 VMEM_LIMIT = 60 * 1024 * 1024
 
 
@@ -89,52 +92,69 @@
     return pl.ds(pl.multiple_of((half * 4 + tensor) * rows, rows), rows)
 
 
+def part_of(r, at, n):
+    return pl.ds(pl.multiple_of(r.start + at, n), n)
+
+
+class Gather:
+    def __init__(self, me, buf, rows, ssem, rsem):
+        def move(k, half, x, dev, at=0, size=rows):
+            r = part_of(block(half, x * 2 + me.c, rows), at, size)
+            return remote(buf.at[r], buf.at[r], ssem.at[k], rsem.at[k], dev)
+
+        n = rows // CHUNKS
+        h, x = me.half, me.x
+        self.me = me
+        self.own_x = move(0, h, x, me.xn())
+        self.own_s = move(1, h, x, me.sib())
+        self.x_s = move(2, h, 1 - x, me.sib())
+        self.z_s = move(3, 1 - h, x, me.sib())
+        self.g_s = move(4, 1 - h, 1 - x, me.sib())
+        self.own_z = [move(5 + i, h, x, me.znb(), i * n, n) for i in range(CHUNKS)]
+        self.z_x = [move(5 + CHUNKS + i, 1 - h, x, me.xn(), i * n, n) for i in range(CHUNKS)]
+
+    def begin(self):
+        for m in self.own_z + [self.own_x, self.own_s]:
+            m.start()
+
+    def finish(self, first, second, fill=()):
+        fill = list(fill)
+
+        def step():
+            if fill:
+                fill.pop(0)()
+
+        step()
+        self.own_x.wait_recv()
+        self.x_s.start()
+        for a, b in zip(self.own_z, self.z_x):
+            a.wait_recv()
+            b.start()
+        self.z_s.start()
+        step()
+        self.own_s.wait_recv()
+        self.x_s.wait_recv()
+        first(self.me.half)
+        for m in self.z_x:
+            m.wait_recv()
+        self.g_s.start()
+        step()
+        self.z_s.wait_recv()
+        self.g_s.wait_recv()
+        second(1 - self.me.half)
+        for m in self.own_z + self.z_x + [self.own_x, self.own_s, self.z_s, self.x_s, self.g_s]:
+            m.wait_send()
+
+
 def gather_acts(me, buf, rows, ssem, rsem, first, second, fill=()):
-    fill = list(fill)
-
-    def step():
-        if fill:
-            fill.pop(0)()
-
-    def move(k, half, x, dev):
-        r = block(half, x * 2 + me.c, rows)
-        return remote(buf.at[r], buf.at[r], ssem.at[k], rsem.at[k], dev)
-
-    h, x = me.half, me.x
-    own_z = move(1, h, x, me.znb())
-    own_x = move(0, h, x, me.xn())
-    own_s = move(2, h, x, me.sib())
-    own_z.start()
-    own_x.start()
-    own_s.start()
-    step()
-    own_x.wait_recv()
-    x_s = move(5, h, 1 - x, me.sib())
-    x_s.start()
-    own_z.wait_recv()
-    z_x = move(3, 1 - h, x, me.xn())
-    z_s = move(4, 1 - h, x, me.sib())
-    z_x.start()
-    z_s.start()
-    step()
-    own_s.wait_recv()
-    x_s.wait_recv()
-    first(h)
-    z_x.wait_recv()
-    g_s = move(6, 1 - h, 1 - x, me.sib())
-    g_s.start()
-    step()
-    z_s.wait_recv()
-    g_s.wait_recv()
-    second(1 - h)
-    for m in (own_x, own_z, own_s, z_x, z_s, x_s, g_s):
-        m.wait_send()
-    while fill:
-        step()
+    g = Gather(me, buf, rows, ssem, rsem)
+    g.begin()
+    g.finish(first, second, fill)
 
 
 def sum_acts(me, part, rows, sib_buf, x_buf, z_buf, ssem, rsem, body, fill=()):
     fill = list(fill)
+    n = rows // CHUNKS
 
     def step():
         if fill:
@@ -148,55 +168,64 @@
         m.start()
         sibs.append(m)
     step()
-    chunk = 64
-
-    def mine(j, i):
+    small = 32
+
+    def mine(j, at, size):
         hh, xx = order[j]
-        return pl.ds(pl.multiple_of((hh * 4 + xx * 2 + me.c) * rows + i * chunk, chunk), chunk)
-
-    def add(j, extra=None):
+        return part_of(block(hh, xx * 2 + me.c, rows), at, size)
+
+    def add(j, at, size, extra=None):
         def go(i):
-            r = mine(j, i)
-            k = pl.ds(pl.multiple_of(i * chunk, chunk), chunk)
+            r = mine(j, at + i * small, small)
+            k = pl.ds(pl.multiple_of(at + i * small, small), small)
             v = part[r, :].astype(F32) + sib_buf[j, k, :].astype(F32)
             if extra is not None:
                 v = v + extra[k, :].astype(F32)
             part[r, :] = v.astype(BF16)
 
-        loop(rows // chunk, go)
-
-    def my_block(j):
-        hh, xx = order[j]
-        return part.at[block(hh, xx * 2 + me.c, rows)]
-
-    to_x = []
-    for j in (0, 1):
-        sibs[j].wait_recv()
-        add(j)
-        m = remote(my_block(j), x_buf.at[j], ssem.at[4 + j], rsem.at[4 + j], me.xn())
-        m.start()
-        to_x.append(m)
+        loop(size // small, go)
+
+    def cut(i):
+        return pl.ds(i * n, n)
+
+    g_x = [
+        remote(part.at[mine(0, i * n, n)], x_buf.at[0, cut(i)], ssem.at[5 + i], rsem.at[5 + i], me.xn())
+        for i in range(CHUNKS)
+    ]
+    x_x = remote(part.at[mine(1, 0, rows)], x_buf.at[1], ssem.at[4], rsem.at[4], me.xn())
+    to_z = [
+        remote(
+            part.at[mine(2, i * n, n)], z_buf.at[cut(i)], ssem.at[5 + CHUNKS + i], rsem.at[5 + CHUNKS + i], me.znb()
+        )
+        for i in range(CHUNKS)
+    ]
+    sibs[0].wait_recv()
+    for i in range(CHUNKS):
+        add(0, i * n, n)
+        g_x[i].start()
+    sibs[1].wait_recv()
+    add(1, 0, rows)
+    x_x.start()
     step()
     sibs[2].wait_recv()
-    to_x[0].wait_recv()
-    add(2, x_buf.at[0])
-    to_z = remote(my_block(2), z_buf, ssem.at[6], rsem.at[6], me.znb())
-    to_z.start()
+    for i in range(CHUNKS):
+        g_x[i].wait_recv()
+        add(2, i * n, n, x_buf.at[0])
+        to_z[i].start()
     sibs[3].wait_recv()
     step()
-    to_x[1].wait_recv()
-    to_z.wait_recv()
-    small = 32
+    x_x.wait_recv()
+    for m in to_z:
+        m.wait_recv()
 
     def last(i):
         k = pl.ds(pl.multiple_of(i * small, small), small)
-        r = pl.ds(pl.multiple_of((h * 4 + x * 2 + me.c) * rows + i * small, small), small)
-        v = part[r, :].astype(F32) + sib_buf[3, k, :].astype(F32)
+        v = part[mine(3, i * small, small), :].astype(F32) + sib_buf[3, k, :].astype(F32)
         v = v + x_buf[1, k, :].astype(F32) + z_buf[k, :].astype(F32)
         body(i * small, small, v)
 
     loop(rows // small, last)
-    for m in sibs + to_x + [to_z]:
+    for m in sibs + g_x + to_z + [x_x]:
         m.wait_send()
     while fill:
         step()
@@ -217,8 +246,8 @@
 
 def forward_kernel(
     dims,
-    tokens, mask, cosine, sine, attn_gain, ffn_gain, w_q, w_k, w_v, w_s, w_o, w_g, w_u, w_d,
-    output, x_mid, mids, wf, s_n, s_nf, s_q, s_k, s_v, s_s, s_m, s_gt, s_g, s_u, s_h, s_p,
+    tokens, cot, mask, cosine, sine, attn_gain, ffn_gain, w_q, w_k, w_v, w_s, w_o, w_g, w_u, w_d,
+    output, x_mid, mids, wf, s_gc, s_n, s_nf, s_q, s_k, s_v, s_s, s_m, s_gt, s_g, s_u, s_h, s_p,
     W, N0, N1, part, sib_buf, x_buf, z_buf, q, k, v, s, m, gt, g, u, h, p,
     zs, zr, ys, yr, lo, ld, ags, agr, rss, rsr, sv,
 ):
@@ -351,9 +380,9 @@
         r = pl.ds(pl.multiple_of(i * small, small), small)
         x = tokens[r, :].astype(F32)
         N0[own_rows(i * small, small), :] = (x * rms(x, EPS) * attn_gain[0:1, :]).astype(BF16)
+        N1[own_rows(i * small, small), :] = cot[r, :]
 
     loop(rows // small, first_norm)
-
     def out_rows(i, src, name):
         def go(j):
             r = pl.ds(pl.multiple_of(i * LEN + j * 256, 256), 256)
@@ -361,33 +390,40 @@
 
         loop(LEN // 256, go)
 
-    def attn_seq(i, l, fetch):
-        def get(name):
-            if fetch:
-                take(l, name)
-
+    def turned(name, dst, i):
         r = seq_rows(i)
-        for name, dst in (("q", q), ("k", k)):
-            get(name)
-            t = dot(N0[r, :], weight(name), NT)
-            half = t.shape[1] // 2
-            t1, t2 = t[:, :half], t[:, half:]
-            c, sn = cosine[...], sine[...]
-            dst[r, :half] = (t1 * c - t2 * sn).astype(BF16)
-            dst[r, half:] = (t2 * c + t1 * sn).astype(BF16)
-        get("v")
+        t = dot(N0[r, :], weight(name), NT)
+        half = t.shape[1] // 2
+        t1, t2 = t[:, :half], t[:, half:]
+        c, sn = cosine[...], sine[...]
+        dst[r, :half] = (t1 * c - t2 * sn).astype(BF16)
+        dst[r, half:] = (t2 * c + t1 * sn).astype(BF16)
+
+    def retain(i):
+        r = seq_rows(i)
         v[r, :] = dot(N0[r, :], weight("v"), NT).astype(BF16)
         raw = dot(q[r, :], k[r, :], NT) * scale
         probs = (raw * mask[i]).astype(BF16)
         p[i] = probs
         m[r, :] = dot(probs, v[r, :])
-        get("s")
+
+    def gate(i):
+        r = seq_rows(i)
         t = dot(N0[r, :], weight("s"), NT)
         s[r, :] = t
         mix = m[r, :]
         gt[r, :] = (jax.nn.silu(t) * (mix * rms(mix, HEAD_FLOOR))).astype(BF16)
-        get("o")
-        out_rows(i, gt, "o")
+
+    stages = (
+        ("q", functools.partial(turned, "q", q)), ("k", functools.partial(turned, "k", k)), ("v", retain),
+        ("s", gate), ("o", lambda i: out_rows(i, gt, "o")),
+    )
+
+    def attn_seq(i, l, fetch):
+        for name, stage in stages:
+            if fetch:
+                take(l, name)
+            stage(i)
 
     def ffn_seq(i, l, fetch):
         r = seq_rows(i)
@@ -406,9 +442,28 @@
     both = lambda body, l: (functools.partial(body, l=l, fetch=True), functools.partial(body, l=l, fetch=False))
 
     for l in range(layers):
-        gather_acts(me, N0, rows, ags.at[2 * l], agr.at[2 * l], *both(attn_seq, l), gfill(2 * l))
+        if l:
+            gather_acts(me, N0, rows, ags.at[2 * l], agr.at[2 * l], *both(attn_seq, l), gfill(2 * l))
+        else:
+            own_rows_of = Gather(me, N0, rows, ags.at[0], agr.at[0])
+            grads_of = Gather(me, N1, rows, ags.at[2 * layers], agr.at[2 * layers])
+            own_rows_of.begin()
+            act(0, 0)()
+            grads_of.begin()
+            idle = lambda i: None
+            own_rows_of.finish(idle, idle, [act(0, 1), act(0, 5), act(2 * layers, 3)])
+            for name, stage in stages:
+                take(0, name)
+                loop(seqs, stage)
+                if name == COT_AFTER:
+                    grads_of.finish(idle, idle, [act(2 * layers, i) for i in (0, 1, 2)])
+                    save(N1, s_gc)
         for src, dst in ((N0, s_n), (q, s_q), (k, s_k), (v, s_v), (p, s_p), (m, s_m), (s, s_s), (gt, s_gt)):
             save(src, dst.at[l])
+
+        if l == 0:
+            saves[0].wait()
+            waited[0] = 1
 
         def to_mid(r0, n, total, l=l):
             r = pl.ds(pl.multiple_of(r0, n), n)
@@ -440,7 +495,7 @@
             y_copy(i, d).wait_send()
 
 
-def run_forward(dims, total, tokens, mask, cosine, sine, attn_gain, ffn_gain, weights):
+def run_forward(dims, total, tokens, cot, mask, cosine, sine, attn_gain, ffn_gain, weights):
     layers, rows, lanes, units, scale = dims
     depth = tokens.shape[1]
     group = 8 * rows
@@ -450,7 +505,8 @@
     hb = pl.BlockSpec(memory_space=pl.ANY)
     outs = [
         ((rows, depth), BF16), ((layers - 1, rows, depth), F32), ((layers, rows, depth), F32),
-        ((layers, total, depth), BF16), ((layers, group, depth), BF16), ((layers, group, depth), BF16),
+        ((layers, total, depth), BF16), ((group, depth), BF16),
+        ((layers, group, depth), BF16), ((layers, group, depth), BF16),
         ((layers, group, qk), BF16), ((layers, group, qk), BF16), ((layers, group, val), BF16),
         ((layers, group, val), F32), ((layers, group, val), F32), ((layers, group, val), BF16),
         ((layers, group, ffn), F32), ((layers, group, ffn), F32), ((layers, group, ffn), BF16),
@@ -461,8 +517,8 @@
     return pl.pallas_call(
         functools.partial(forward_kernel, dims),
         out_shape=[jax.ShapeDtypeStruct(s, d) for s, d in outs],
-        in_specs=[vm] * 6 + [hb] * 8,
-        out_specs=[vm] * 3 + [hb] * 13,
+        in_specs=[vm] * 7 + [hb] * 8,
+        out_specs=[vm] * 3 + [hb] * 14,
         scratch_shapes=[
             pltpu.VMEM((total, depth), BF16),
             pltpu.VMEM((group, depth), BF16), pltpu.VMEM((group, depth), BF16), pltpu.VMEM((group, depth), BF16),
@@ -473,11 +529,11 @@
             pltpu.VMEM((seqs, LEN, LEN), BF16),
             dma((n_groups, 3)), dma((n_groups, 3)), dma((n_groups, 4)), dma((n_groups, 4)),
             dma((n_groups,)), dma((n_groups,)),
-            dma((2 * layers, 7)), dma((2 * layers, 7)), dma((2 * layers, 7)), dma((2 * layers, 7)),
-            dma((12 * layers,)),
+            *[dma((2 * layers + 1, 5 + 2 * CHUNKS)) for _ in range(4)],
+            dma((12 * layers + 1,)),
         ],
         compiler_params=pltpu.CompilerParams(collective_id=0, has_side_effects=True, vmem_limit_bytes=VMEM_LIMIT),
-    )(tokens, mask, cosine, sine, attn_gain, ffn_gain, *weights)
+    )(tokens, cot, mask, cosine, sine, attn_gain, ffn_gain, *weights)
 
 
 SLOTS = 4
@@ -492,7 +548,7 @@
 def backward_kernel(
     dims,
     cot, tokens, x_mid, mids, mask, cosine, sine, attn_gain, ffn_gain,
-    wf, s_n, s_nf, s_q, s_k, s_v, s_s, s_m, s_gt, s_g, s_u, s_h, s_p,
+    wf, s_gc, s_n, s_nf, s_q, s_k, s_v, s_s, s_m, s_gt, s_g, s_u, s_h, s_p,
     input_grad, gains, rz,
     gr, xb, nb, ga0, ga1, part, sib_buf, x_buf, z_buf, W, a1, a2, a3, q, k, v, p, t1, t2, tq, tk, G, ry, acc, acc_in,
     ys, yr, zs, zr, os, ags, agr, rss, rsr, ld, gns, gnr, credit,
@@ -640,6 +696,7 @@
         return e * gx - (e * e * e) * x * (inner / depth)
 
     me.greet()
+    load("gc", s_gc, ga0)
     load_ffn(order[0])
     load_mid(order[0])
     load_h(order[0])
@@ -649,7 +706,6 @@
     def begin(i):
         r = pl.ds(pl.multiple_of(i * small, small), small)
         gr[r, :] = cot[r, :].astype(F32)
-        ga0[own_rows(i * small, small), :] = cot[r, :]
 
     loop(rows // small, begin)
 
@@ -771,7 +827,12 @@
     for at, l in enumerate(order):
         last = at == layers - 1
         first = after([("wf", l), ("g", l), ("u", l), ("mid", l)], ffn_seq)
-        gather_acts(me, ga0, rows, ags.at[2 * at], agr.at[2 * at], first, ffn_seq, gfill(2 * at))
+        if at == 0:
+            ready("gc")
+            first(0)
+            ffn_seq(1)
+        else:
+            gather_acts(me, ga0, rows, ags.at[2 * at], agr.at[2 * at], first, ffn_seq, gfill(2 * at))
         load_attn(l)
         open_to[0] = 8 * at + 3
 
@@ -841,7 +902,7 @@
     return pl.pallas_call(
         functools.partial(backward_kernel, dims),
         out_shape=[jax.ShapeDtypeStruct(s, d) for s, d in outs],
-        in_specs=[vm, vm, hb, hb] + [vm] * 5 + [hb] * 13,
+        in_specs=[vm, vm, hb, hb] + [vm] * 5 + [hb] * 14,
         out_specs=[vm] * 2 + [hb],
         scratch_shapes=[
             pltpu.VMEM((rows, depth), F32), pltpu.VMEM((rows, depth), F32), big, big, big, big,
@@ -855,8 +916,8 @@
             pltpu.VMEM((SLOTS, most, depth), BF16), pltpu.VMEM((SLOTS, most, depth // 2), BF16),
             pltpu.VMEM((6, 8, depth), F32), pltpu.VMEM((5, 8, depth), F32),
             dma((jobs, 4)), dma((jobs, 4)), dma((jobs, 3)), dma((jobs, 3)), dma((jobs,)),
-            dma((2 * layers, 7)), dma((2 * layers, 7)), dma((2 * layers, 7)), dma((2 * layers, 7)),
-            dma((16 * layers,)), dma((5,)), dma((5,)), pltpu.SemaphoreType.REGULAR((SLOTS,)),
+            *[dma((2 * layers, 5 + 2 * CHUNKS)) for _ in range(4)],
+            dma((16 * layers + 1,)), dma((5,)), dma((5,)), pltpu.SemaphoreType.REGULAR((SLOTS,)),
         ],
         compiler_params=pltpu.CompilerParams(collective_id=1, has_side_effects=True, vmem_limit_bytes=VMEM_LIMIT),
     )(cot, tokens, x_mid, mids, mask, cosine, sine, attn_gain, ffn_gain, *kept)
@@ -1229,7 +1290,7 @@
     )
     dims = (layers, tokens.shape[0], w_query.shape[1], units, HEAD_QK ** (-0.5))
     output, x_mid, mids, *kept = run_forward(
-        dims, total, tokens, mask, cosine, sine, attn_gain, ffn_gain, weights
+        dims, total, tokens, cotangent, mask, cosine, sine, attn_gain, ffn_gain, weights
     )
     input_grad, gains, parts = run_backward(
         dims, cotangent, tokens, x_mid, mids, mask, cosine, sine, attn_gain, ffn_gain, kept

time: 784 us -> 756 us (0.964)
  Pallas kernels: 758 us -> 733 us
    pallas_call x1, Pallas kernels: 365 us -> 348 us  [run_backward(): pl.pallas_call(functools.partial(backward_kernel, dims), out_shape=[jax.S...]
where the time goes in v3:
time: 756 us; the launch traced here: 747 us
  Pallas kernels  733 us (97%)
    pallas_call x1, Pallas kernels, run_forward(): pl.pallas_call(functools.partial(forward_kernel, dims), out_shape=[jax.Sh...  376 us
    pallas_call x1, Pallas kernels, run_backward(): pl.pallas_call(functools.partial(backward_kernel, dims), out_shape=[jax.S...  348 us
  transfers between devices with their start and end apart: 1, of which 0 were waited for; matrix products, arithmetic and copies ran while one was open for 1% of the time, Pallas kernels for 0%

profile of v3, /device:TPU:0, one launch (start us, length us, event | category | flops | bytes accessed | tf_op | source)
XLA Modules:
  0.0 746.9 jit_solution(3225804560790518323)
XLA Ops:
  0.6 0.0 copy-start.4
  0.7 0.0 copy-start.1
  0.7 0.0 copy-start.2
  0.7 3.1 collective-permute-start
  3.9 1.7 fusion.1
  5.6 0.2 multiply_exponential_fusion
  5.8 0.1 fusion
  5.9 0.0 copy-done.1
  5.9 1.0 copy.25
  6.9 0.0 copy-done.2
  6.9 1.0 copy.26
  7.9 0.0 collective-permute-done
  7.9 0.0 copy-done.4
  7.9 1.8 and_select_fusion.mask
  9.7 375.9 %shard_map.220 = (bf16[128,2048]{1,0:T(8,128)(2,1)}, f32[1,128,2048]{2,1,0:T(8,128)}, f32[2,128,2048]{2,1,0:T(8,128)}, bf16[2,3104,2048]{2,1,0:T(8,128)(2,1)}, b...) custom-call(bf16[128,2048]{1,0:T(8,128)(2,1)} %tokens.3, ...), custom_call_target="tpu_custom_call" | custom-call | tf_op jit(solution)/shard_map/pallas_call | solution.py:517
  385.5 348.2 %shard_map.221 = (f32[128,2048]{1,0:T(8,128)}, f32[8,2048]{1,0:T(8,128)}, bf16[2,2,2,3104,256]{4,3,2,1,0:T(8,128)(2,1)}) custom-call(bf16[128,2048]{1,0:T(8,128)(2,1)} %cot.3, bf16[128,2048]{1,0:T(8,128)(2,1)} %tokens.3, f32[1,128,2048]{2,1,0:T(8,128)} %get-tuple-element.41.x_mid, f32[2,128,2048]{2,1,0:T(8,128)} %get-tuple-element.42.mids, ...), custom_call_target="tpu_custom_call" | custom-call | tf_op jit(solution)/shard_map/pallas_call | solution.py:902
  733.7 1.5 fusion.3
  735.3 0.0 copy-start.3
  735.3 0.0 copy-start
  735.3 9.4 %shard_map.222 = (f32[2,256,512]{2,1,0:T(8,128)}, f32[2,256,512]{2,1,0:T(8,128)}, f32[2,864,256]{2,1,0:T(8,128)}, f32[2,864,256]{2,1,0:T(8,128)}, f32[2,864,256]...) custom-call(bf16[2,2,2,3104,256]{4,3,2,1,0:T(8,128)(2,1)} %get-tuple-element.59.parts), custom_call_target="tpu_custom_call" | custom-call | tf_op jit(solution)/shard_map/pallas_call | solution.py:952
  744.7 0.0 copy-done.3
  744.7 0.8 copy.29
  745.5 0.0 copy-done
  745.5 1.0 copy.30
  (2 shorter events, 0.0 us)
Async XLA Ops:
  0.6 7.3 copy-start.4
  0.7 5.2 copy-start.1
  0.7 6.2 copy-start.2
  0.7 7.2 collective-permute-start
  735.3 9.4 %copy-start.3 = (bf16[128,2048]{1,0:T(8,128)(2,1)S(1)}, bf16[128,2048]{1,0:T(8,128)(2,1)}, u32[]{:S(2)}) copy-start(bf16[128,2048]{1,0:T(8,128)(2,1)} %get-tuple-element.84) | copy-start | bytes 1572868
  735.3 10.2 %copy-start = (f32[128,2048]{1,0:T(8,128)S(1)}, f32[128,2048]{1,0:T(8,128)}, u32[]{:S(2)}) copy-start(f32[128,2048]{1,0:T(8,128)} %get-tuple-element.85) | copy-start | bytes 3145732

commit v4 on v3

--- a/solution.py
+++ b/solution.py
@@ -23,7 +23,7 @@
 SCHED = (
     ("III", "P", "", "PI", "PI", "PI"),
     ("PI", "PI", "", "PI", "PI", ""),
-    ("PI", "PI", "", "PI", "PI", ""),
+    ("PI", "PI", "", "PI", "PI", "PI"),
     ("PI", "PI", "", "PI", "PI", ""),
     ("PI", "PI", "", "", ""),
 )
@@ -537,11 +537,12 @@
 
 
 SLOTS = 4
+EARLY = 1
 BSCHED = (
     ("", "", "", "", "M", "MM", ""),
-    ("C", "C", "", "", "CMM", "CMCMM", ""),
+    ("C", "C", "", "", "CMM", "CMCM", ""),
     ("C", "C", "C", "", "M", "MM", ""),
-    ("C", "C", "", "", "CMM", "CMCMM", ""),
+    ("C", "C", "", "", "CMM", "CMCM", ""),
 )
 
 
@@ -560,7 +561,7 @@
     small = 32
     seqs = 2
     order = list(reversed(range(layers)))
-    jobs = [(l, n) for l in order for n in ("d", "g", "u", "o", "q", "k", "v", "s")]
+    jobs = [(l, n) for l in order for n in ("d", "g", "u", "o", "s", "q", "k", "v")]
     index = {job: i for i, job in enumerate(jobs)}
     own = (me.half * 4 + me.tensor) * rows
     ffn_row = units["g"][0]
@@ -714,10 +715,10 @@
         "g": (t1, nb, ("nf",), None),
         "u": (t2, nb, (), lambda l: load_n(l)),
         "o": (a3, ga1, ("gt",), None),
-        "q": (tq, nb, ("n",), None),
+        "s": (t2, nb, ("n",), None),
+        "q": (tq, nb, (), None),
         "k": (tk, nb, (), None),
-        "v": (t1, nb, (), None),
-        "s": (t2, nb, (), lambda l: (load_nf(l - 1), load_h(l - 1)) if l else None),
+        "v": (t1, nb, (), lambda l: (load_nf(l - 1), load_h(l - 1)) if l else None),
     }
     open_to, made, added = [0], [0], [0]
 
@@ -816,6 +817,12 @@
         attn_head(i)
         attn_tail(i)
 
+    def attn_second(i, at):
+        attn_head(i)
+        open_to[0] = 8 * at + 3 + EARLY
+        make_all()
+        attn_tail(i)
+
     def after(keys, body):
         def go(i):
             make_all()
@@ -846,7 +853,7 @@
         if l:
             load(("x", l), x_mid.at[l - 1], xb)
         first = after([(key, l) for key in ("wa", "s", "m", "q", "k", "v", "p") + (("x",) if l else ())], attn_seq)
-        gather_acts(me, ga1, rows, ags.at[2 * at + 1], agr.at[2 * at + 1], first, attn_seq, gfill(2 * at + 1))
+        gather_acts(me, ga1, rows, ags.at[2 * at + 1], agr.at[2 * at + 1], first, functools.partial(attn_second, at=at), gfill(2 * at + 1))
         if not last:
             load_ffn(order[at + 1])
         open_to[0] = 8 * at + 8

time: 756 us -> 752 us (level)
  no operation moved by 1% of the time
where the time goes in v4:
time: 752 us; the launch traced here: 741 us
  Pallas kernels  727 us (97%)
    pallas_call x1, Pallas kernels, run_forward(): pl.pallas_call(functools.partial(forward_kernel, dims), out_shape=[jax.Sh...  374 us
    pallas_call x1, Pallas kernels, run_backward(): pl.pallas_call(functools.partial(backward_kernel, dims), out_shape=[jax.S...  344 us
  transfers between devices with their start and end apart: 1, of which 0 were waited for; matrix products, arithmetic and copies ran while one was open for 1% of the time, Pallas kernels for 0%

profile of v4, /device:TPU:0, one launch (start us, length us, event | category | flops | bytes accessed | tf_op | source)
XLA Modules:
  0.0 740.6 jit_solution(3321640876003196163)
XLA Ops:
  0.6 0.0 copy-start.4
  0.7 0.0 copy-start.1
  0.7 0.0 copy-start.2
  0.7 3.1 collective-permute-start
  3.9 1.7 fusion.1
  5.6 0.2 multiply_exponential_fusion
  5.8 0.1 fusion
  5.9 0.0 copy-done.1
  5.9 1.0 copy.25
  6.9 0.0 copy-done.2
  6.9 1.0 copy.26
  7.9 0.0 collective-permute-done
  7.9 0.0 copy-done.4
  7.9 1.8 and_select_fusion.mask
  9.7 373.6 %shard_map.220 = (bf16[128,2048]{1,0:T(8,128)(2,1)}, f32[1,128,2048]{2,1,0:T(8,128)}, f32[2,128,2048]{2,1,0:T(8,128)}, bf16[2,3104,2048]{2,1,0:T(8,128)(2,1)}, b...) custom-call(bf16[128,2048]{1,0:T(8,128)(2,1)} %tokens.3, ...), custom_call_target="tpu_custom_call" | custom-call | tf_op jit(solution)/shard_map/pallas_call | solution.py:517
  383.3 344.2 %shard_map.221 = (f32[128,2048]{1,0:T(8,128)}, f32[8,2048]{1,0:T(8,128)}, bf16[2,2,2,3104,256]{4,3,2,1,0:T(8,128)(2,1)}) custom-call(bf16[128,2048]{1,0:T(8,128)(2,1)} %cot.3, bf16[128,2048]{1,0:T(8,128)(2,1)} %tokens.3, f32[1,128,2048]{2,1,0:T(8,128)} %get-tuple-element.41.x_mid, f32[2,128,2048]{2,1,0:T(8,128)} %get-tuple-element.42.mids, ...), custom_call_target="tpu_custom_call" | custom-call | tf_op jit(solution)/shard_map/pallas_call | solution.py:909
  727.5 1.5 fusion.3
  729.0 0.0 copy-start.3
  729.0 0.0 copy-start
  729.0 9.4 %shard_map.222 = (f32[2,256,512]{2,1,0:T(8,128)}, f32[2,256,512]{2,1,0:T(8,128)}, f32[2,864,256]{2,1,0:T(8,128)}, f32[2,864,256]{2,1,0:T(8,128)}, f32[2,864,256]...) custom-call(bf16[2,2,2,3104,256]{4,3,2,1,0:T(8,128)(2,1)} %get-tuple-element.59.parts), custom_call_target="tpu_custom_call" | custom-call | tf_op jit(solution)/shard_map/pallas_call | solution.py:959
  738.4 0.0 copy-done.3
  738.4 0.8 copy.29
  739.2 0.0 copy-done
  739.2 1.0 copy.30
  (2 shorter events, 0.0 us)
Async XLA Ops:
  0.6 7.3 copy-start.4
  0.7 5.2 copy-start.1
  0.7 6.2 copy-start.2
  0.7 7.2 collective-permute-start
  729.0 9.4 %copy-start.3 = (bf16[128,2048]{1,0:T(8,128)(2,1)S(1)}, bf16[128,2048]{1,0:T(8,128)(2,1)}, u32[]{:S(2)}) copy-start(bf16[128,2048]{1,0:T(8,128)(2,1)} %get-tuple-element.84) | copy-start | bytes 1572868
  729.0 10.2 %copy-start = (f32[128,2048]{1,0:T(8,128)S(1)}, f32[128,2048]{1,0:T(8,128)}, u32[]{:S(2)}) copy-start(f32[128,2048]{1,0:T(8,128)} %get-tuple-element.85) | copy-start | bytes 3145732

commit v5 on v4

--- a/solution.py
+++ b/solution.py
@@ -28,7 +28,7 @@
     ("PI", "PI", "", "", ""),
 )
 COT_AFTER = "v"
-CHUNKS = 2
+CHUNKS = 4
 VMEM_LIMIT = 60 * 1024 * 1024
 
 

time: 752 us -> 753 us (level)
  no operation moved by 1% of the time
where the time goes in v5:
time: 753 us; the launch traced here: 743 us
  Pallas kernels  730 us (97%)
    pallas_call x1, Pallas kernels, run_forward(): pl.pallas_call(functools.partial(forward_kernel, dims), out_shape=[jax.Sh...  375 us
    pallas_call x1, Pallas kernels, run_backward(): pl.pallas_call(functools.partial(backward_kernel, dims), out_shape=[jax.S...  346 us
  transfers between devices with their start and end apart: 1, of which 0 were waited for; matrix products, arithmetic and copies ran while one was open for 1% of the time, Pallas kernels for 0%

profile of v5, /device:TPU:0, one launch (start us, length us, event | category | flops | bytes accessed | tf_op | source)
XLA Modules:
  0.0 743.4 jit_solution(12403635125381451899)
XLA Ops:
  0.6 0.0 copy-start.4
  0.7 0.0 copy-start.1
  0.7 0.0 copy-start.2
  0.7 3.1 collective-permute-start
  3.9 1.7 fusion.1
  5.6 0.2 multiply_exponential_fusion
  5.8 0.1 fusion
  5.9 0.0 copy-done.1
  5.9 1.0 copy.25
  6.9 0.0 copy-done.2
  6.9 1.0 copy.26
  7.9 0.0 collective-permute-done
  7.9 0.0 copy-done.4
  7.9 1.8 and_select_fusion.mask
  9.7 374.5 %shard_map.220 = (bf16[128,2048]{1,0:T(8,128)(2,1)}, f32[1,128,2048]{2,1,0:T(8,128)}, f32[2,128,2048]{2,1,0:T(8,128)}, bf16[2,3104,2048]{2,1,0:T(8,128)(2,1)}, b...) custom-call(bf16[128,2048]{1,0:T(8,128)(2,1)} %tokens.3, ...), custom_call_target="tpu_custom_call" | custom-call | tf_op jit(solution)/shard_map/pallas_call | solution.py:517
  384.2 346.0 %shard_map.221 = (f32[128,2048]{1,0:T(8,128)}, f32[8,2048]{1,0:T(8,128)}, bf16[2,2,2,3104,256]{4,3,2,1,0:T(8,128)(2,1)}) custom-call(bf16[128,2048]{1,0:T(8,128)(2,1)} %cot.3, bf16[128,2048]{1,0:T(8,128)(2,1)} %tokens.3, f32[1,128,2048]{2,1,0:T(8,128)} %get-tuple-element.41.x_mid, f32[2,128,2048]{2,1,0:T(8,128)} %get-tuple-element.42.mids, ...), custom_call_target="tpu_custom_call" | custom-call | tf_op jit(solution)/shard_map/pallas_call | solution.py:909
  730.2 1.5 fusion.3
  731.8 0.0 copy-start.3
  731.8 0.0 copy-start
  731.8 9.4 %shard_map.222 = (f32[2,256,512]{2,1,0:T(8,128)}, f32[2,256,512]{2,1,0:T(8,128)}, f32[2,864,256]{2,1,0:T(8,128)}, f32[2,864,256]{2,1,0:T(8,128)}, f32[2,864,256]...) custom-call(bf16[2,2,2,3104,256]{4,3,2,1,0:T(8,128)(2,1)} %get-tuple-element.59.parts), custom_call_target="tpu_custom_call" | custom-call | tf_op jit(solution)/shard_map/pallas_call | solution.py:959
  741.2 0.0 copy-done.3
  741.2 0.8 copy.29
  742.0 0.0 copy-done
  742.0 1.0 copy.30
  (2 shorter events, 0.0 us)
Async XLA Ops:
  0.6 7.3 copy-start.4
  0.7 5.2 copy-start.1
  0.7 6.2 copy-start.2
  0.7 7.2 collective-permute-start
  731.8 9.4 %copy-start.3 = (bf16[128,2048]{1,0:T(8,128)(2,1)S(1)}, bf16[128,2048]{1,0:T(8,128)(2,1)}, u32[]{:S(2)}) copy-start(bf16[128,2048]{1,0:T(8,128)(2,1)} %get-tuple-element.84) | copy-start | bytes 1572868
  731.8 10.2 %copy-start = (f32[128,2048]{1,0:T(8,128)S(1)}, f32[128,2048]{1,0:T(8,128)}, u32[]{:S(2)}) copy-start(f32[128,2048]{1,0:T(8,128)} %get-tuple-element.85) | copy-start | bytes 3145732
